TPU v7x, 32 devices: a whole 2x2x4 slice. The times are simulated.
32 devices in a mesh: group: 1, expert: 32 (over z, y, x, core).
Axes of the slice: x: 2, y: 2, z: 4, core: 2. Of those that a mesh axis runs over, the one named last changes fastest.
Arguments:
- text_rows: bfloat16 [2048, 2560], P(('group', 'expert')), may hold values from -6 to 6
- image_rows: bfloat16 [64, 16, 2560], P(('group', 'expert')), may hold values from -6 to 6
- image_probe: bfloat16 [2560], replicated, may hold values from -0.125 to 0.125
- response_image: int32 [128], P(('group', 'expert')), may hold values from 0 to 63
- token_response: int32 [32, 64], P(('group', 'expert')), may hold values from 0 to 3, never falling along the last dimension, each value on 1 to 32 neighbouring positions
- norm_gain: bfloat16 [2560], replicated, may hold values from 0.5 to 1.5
- router_weight: bfloat16 [2560, 16], replicated, may hold values from -0.125 to 0.125
- expert_routes: int32 [2048, 6], P(('group', 'expert')), may hold values from 0 to 15, all different within a row; in each aligned block of 64 rows (0 to 63, 64 to 127, ...) at most 32 rows name the same one
- gate_weight: bfloat16 [32, 768, 2560], P('expert'), may hold values from -0.125 to 0.125
- up_weight: bfloat16 [32, 768, 2560], P('expert'), may hold values from -0.125 to 0.125
- down_weight: bfloat16 [32, 768, 2560], P('expert'), may hold values from -0.15625 to 0.15625
- reward_head: bfloat16 [2560], replicated, may hold values from -0.125 to 0.125
Outputs:
- token_output: bfloat16 [2048, 2560], P(('group', 'expert'))
- response_score: float32 [128], P(('group', 'expert'))
Inputs may be any that keep to these rules, and one draw needn't show every extreme that they name: `expert_routes`: each row names 6 different experts. In the rows of one device, no expert is named by more than 32 rows, and in some device's rows some expert is named by exactly 32. `token_response`: along each device's row the value never falls; every response of the device has 1 to 32 tokens.
All inputs are finite; a program needn't handle non-finite values.
Results may differ from a plain program's by a relative error of at most 0.0046.
Values may be sent and summed in bfloat16 or wider, within the bound.
A program may use at most 64 MiB of HBM per device.

v0:
```python
import math

import jax
import jax.numpy as jnp
from jax import lax
from jax.sharding import PartitionSpec as P

epsilon = 1e-06


def expert_half(arrived, gate_rows, up_rows, down_rows):
    sources, slot_count, feature_count = arrived.shape
    inputs = arrived.reshape(sources * slot_count, feature_count)
    contract = (((1,), (1,)), ((), ()))
    gate_value = lax.dot_general(inputs, gate_rows, contract, preferred_element_type=jnp.float32)
    up_value = lax.dot_general(inputs, up_rows, contract, preferred_element_type=jnp.float32)
    active = (jax.nn.silu(gate_value) * up_value).astype(jnp.bfloat16)
    result = jnp.dot(active, down_rows, preferred_element_type=jnp.float32).astype(jnp.bfloat16)
    return result.reshape(sources, slot_count, feature_count)


def body(
    text_rows,
    image_rows,
    image_probe,
    response_image,
    token_response,
    norm_gain,
    router_weight,
    expert_routes,
    gate_weight,
    up_weight,
    down_weight,
    reward_head,
):
    token_count, feature_count = text_rows.shape
    top_count = expert_routes.shape[1]
    expert_count = router_weight.shape[1]
    capacity = min(token_count, 4 * token_count * top_count // (3 * expert_count))
    device_count = lax.axis_size("expert")
    response_count = response_image.shape[0]
    probe_score = jnp.einsum(
        "ivd,d->iv", image_rows, image_probe, preferred_element_type=jnp.float32
    )
    pool_weight = jax.nn.sigmoid(probe_score).astype(jnp.bfloat16)
    pooled_sum = jnp.einsum(
        "iv,ivd->id", pool_weight, image_rows, preferred_element_type=jnp.float32
    )
    pooled = (pooled_sum / math.sqrt(image_rows.shape[1])).astype(jnp.bfloat16)
    shard_rows = lax.all_gather(pooled, "expert", axis=0, tiled=True)
    image_ids = jnp.arange(shard_rows.shape[0], dtype=jnp.int32)
    choose = (response_image[:, None] == image_ids[None, :]).astype(jnp.bfloat16)
    response_context = jnp.dot(choose, shard_rows, preferred_element_type=jnp.float32).astype(
        jnp.bfloat16
    )
    response_onehot = (
        token_response[0][:, None] == jnp.arange(response_count, dtype=jnp.int32)[None, :]
    )
    token_context = jnp.dot(
        response_onehot.astype(jnp.bfloat16), response_context, preferred_element_type=jnp.float32
    )
    hidden_state = text_rows.astype(jnp.float32) + token_context
    inverse = lax.rsqrt(jnp.mean(hidden_state * hidden_state, axis=-1, keepdims=True) + epsilon)
    normed = (hidden_state * inverse * norm_gain.astype(jnp.float32)).astype(jnp.bfloat16)
    logits = jnp.dot(normed, router_weight, preferred_element_type=jnp.float32)
    expert_ids = jnp.arange(expert_count, dtype=jnp.int32)
    route_match = expert_routes[:, :, None] == expert_ids[None, None, :]
    chosen = jax.nn.sigmoid(jnp.sum(jnp.where(route_match, logits[:, None, :], 0.0), axis=2))
    route_weight = chosen / jnp.sum(chosen, axis=1, keepdims=True)
    routed = expert_routes.reshape(-1)
    member = (routed[:, None] == expert_ids[None, :]).astype(jnp.int32)
    earlier = jnp.cumsum(member, axis=0) - member
    places = routed * capacity + jnp.sum(earlier * member, axis=1)
    owners = jnp.arange(routed.shape[0], dtype=jnp.int32) // top_count + 1
    slot_token = jnp.zeros((expert_count * capacity,), jnp.int32).at[places].set(owners)
    padded = jnp.concatenate([jnp.zeros((1, feature_count), jnp.bfloat16), normed], axis=0)
    outgoing = padded[slot_token]
    doubled = jnp.broadcast_to(
        outgoing.reshape(expert_count, 1, capacity, feature_count),
        (expert_count, 2, capacity, feature_count),
    )
    partials = expert_half(
        lax.all_to_all(
            doubled.reshape(device_count, capacity, feature_count),
            "expert",
            split_axis=0,
            concat_axis=0,
            tiled=True,
        ),
        gate_weight[0],
        up_weight[0],
        down_weight[0],
    )
    returned = lax.all_to_all(partials, "expert", split_axis=0, concat_axis=0, tiled=True)
    both_halves = returned.reshape(expert_count, 2, capacity, feature_count).astype(jnp.float32)
    outputs = (
        (both_halves[:, 0] + both_halves[:, 1])
        .astype(jnp.bfloat16)
        .reshape(expert_count * capacity, feature_count)
    )
    gathered = outputs[places].reshape(token_count, top_count, feature_count).astype(jnp.float32)
    mixture = jnp.sum(route_weight[:, :, None] * gathered, axis=1)
    combined = hidden_state + mixture
    reward = jnp.sum(combined * reward_head.astype(jnp.float32), axis=-1)
    totals = jnp.sum(jnp.where(response_onehot, reward[:, None], 0.0), axis=0)
    counts = jnp.sum(response_onehot.astype(jnp.float32), axis=0)
    return (combined.astype(jnp.bfloat16), totals / counts)


def solution(mesh):
    in_specs = (
        P(("group", "expert"), None),
        P(("group", "expert"), None, None),
        P(),
        P(("group", "expert")),
        P(("group", "expert"), None),
        P(),
        P(),
        P(("group", "expert"), None),
        P("expert", None, None),
        P("expert", None, None),
        P("expert", None, None),
        P(),
    )
    out_specs = (P(("group", "expert"), None), P(("group", "expert")))
    return jax.shard_map(body, mesh=mesh, in_specs=in_specs, out_specs=out_specs, check_vma=False)
```

profile of v0, /device:TPU:0, one launch (start us, length us, event | category | flops | bytes accessed | tf_op | source)
XLA Modules:
  0.0 331.0 jit_solution(9250015458060324065)
XLA Ops:
  0.7 0.7 broadcast_multiply_fusion
  1.4 0.8 copy.36
  2.4 0.7 reshape.142
  3.4 0.7 convert_element_type.65
  4.6 0.9 reduce-window.6
  5.9 2.9 scatter_custom_fusion
  8.8 44.1 %all-gather = bf16[32,2,2560]{2,1,0:T(2,128)(2,1)S(1)} all-gather(bf16[1,2,2560]{2,1,0:T(2,128)(2,1)S(1)} %fusion.14), channel_id=1, replica_groups=mesh['group'=1,'expert'=32] {'expert'}, dimensions={0}, use_global_device_ids=true | all-gather | bytes 337920 | tf_op jit(solution)/shard_map/all_gather | solution.py:50
  53.0 1.5 multiply_reduce_fusion.2
  54.7 0.7 copy-done.1
  55.5 2.6 gather_fusion
  58.2 0.6 broadcast_in_dim.30
  58.8 118.1 %all_to_all.10 = bf16[32,32,2560]{2,1,0:T(8,128)(2,1)S(1)} all-to-all(bf16[32,32,2560]{2,1,0:T(8,128)(2,1)S(1)} %bitcast.72), channel_id=1, replica_groups=mesh['group'=1,'expert'=32] {'expert'}, dimensions={0} | all-to-all | bytes 10485760 | tf_op jit(solution)/shard_map/all_to_all | solution.py:83
  176.9 4.3 %fusion.3 = f32[1024,768]{1,0:T(8,128)S(1)} fusion(bf16[1024,2560]{1,0:T(8,128)(2,1)S(1)} %bitcast.75, bf16[1,768,2560]{2,1,0:T(8,128)(2,1)S(1)} %copy-done.7), kind=kOutput, calls=%fused_computation.10 | convolution fusion | flops 4026531840 | bytes 12320768 | tf_op jit(solution)/shard_map/dot_general | solution.py:16
  181.2 4.6 %multiply_convert_fusion = bf16[1024,768]{1,0:T(8,128)(2,1)S(1)} fusion(f32[1024,768]{1,0:T(8,128)S(1)} %fusion.3, bf16[1024,2560]{1,0:T(8,128)(2,1)S(1)} %bitcast.76, bf16[1,768,2560]{2,1,0:T(8,128)(2,1)S(1)} %copy-done.8), kind=kOutput, calls=%fused_computation.16 | convolution fusion | flops 4031250432 | bytes 13893632 | tf_op jit(solution)/shard_map/dot_general | solution.py:15
  185.8 6.0 %convolution_convert_fusion = bf16[1024,2560]{1,0:T(8,128)(2,1)} fusion(bf16[1024,768]{1,0:T(8,128)(2,1)S(1)} %multiply_convert_fusion, bf16[1,768,2560]{2,1,0:T(8,128)(2,1)S(1)} %copy-done.9), kind=kOutput, calls=%fused_computation.3 | convolution fusion | flops 4029153280 | bytes 10747904 | tf_op jit(solution)/shard_map/dot_general | solution.py:18
  191.8 4.0 %all-to-all-start.1 = ((bf16[32,32,2560]{2,1,0:T(8,128)(2,1)}), bf16[32,32,2560]{2,1,0:T(8,128)(2,1)}, u32[]{:S(2)}, u32[]{:S(2)}) async-start(bf16[32,32,2560]{2,1,0:T(8,128)(2,1)} %bitcast.74), calls=%async_computation.1 | async-start | bytes 10485760 | tf_op jit(solution)/shard_map/all_to_all | solution.py:94
  196.2 116.2 %all-to-all-done.1 = bf16[32,32,2560]{2,1,0:T(8,128)(2,1)} async-done(((bf16[32,32,2560]{2,1,0:T(8,128)(2,1)}), bf16[32,32,2560]{2,1,0:T(8,128)(2,1)}, u32[]{:S(2)}, u32[]{:S(2)}) %all-to-all-start.1) | async-done | bytes 5242912 | tf_op jit(solution)/shard_map/all_to_all | solution.py:94
  312.4 3.9 %convert.2 = f32[16,2,32,2560]{3,2,1,0:T(8,128)S(1)} convert(bf16[16,2,32,2560]{3,2,1,0:T(8,128)(2,1)} %bitcast.15) | non-fusion elementwise | flops 2621440 | bytes 15728640 | tf_op jit(solution)/shard_map/convert_element_type | solution.py:95
  316.3 0.7 fusion.1
  317.1 3.3 gather_fusion.1
  320.3 4.5 %reshape.114 = f32[64,6,2560]{2,1,0:T(8,128)} reshape(bf16[384,2560]{1,0:T(8,128)(2,1)} %gather_fusion.1) | data formatting | bytes 5898240 | tf_op jit(solution)/shard_map/convert_element_type | solution.py:101
  324.8 4.5 %multiply_reduce_fusion = f32[64,2560]{1,0:T(8,128)S(1)} fusion(f32[64,6,2560]{2,1,0:T(8,128)} %reshape.114, f32[64,6]{1,0:T(8,128)S(1)} %copy.34), kind=kLoop, calls=%fused_computation.8 | loop fusion | flops 1802240 | bytes 4589056 | tf_op jit(solution)/shard_map/reduce_sum | solution.py:102
  329.4 0.9 multiply_reduce_fusion.1
  330.4 0.5 div.53
  (47 shorter events, 2.3 us)
Async XLA Ops:
  0.6 2.5 copy-start
  54.6 0.9 copy-start.1
  58.7 118.1 %copy-start.7 = (bf16[1,768,2560]{2,1,0:T(8,128)(2,1)S(1)}, bf16[1,768,2560]{2,1,0:T(8,128)(2,1)}, u32[]{:S(2)}) copy-start(bf16[1,768,2560]{2,1,0:T(8,128)(2,1)} %param.21) | copy-start | bytes 11796484
  176.9 4.3 %copy-start.8 = (bf16[1,768,2560]{2,1,0:T(8,128)(2,1)S(1)}, bf16[1,768,2560]{2,1,0:T(8,128)(2,1)}, u32[]{:S(2)}) copy-start(bf16[1,768,2560]{2,1,0:T(8,128)(2,1)} %param.20) | copy-start | bytes 11796484
  181.2 4.6 %copy-start.9 = (bf16[1,768,2560]{2,1,0:T(8,128)(2,1)S(1)}, bf16[1,768,2560]{2,1,0:T(8,128)(2,1)}, u32[]{:S(2)}) copy-start(bf16[1,768,2560]{2,1,0:T(8,128)(2,1)} %param.22) | copy-start | bytes 11796484
  191.8 4.0 %copy-start.5 = (bf16[2560]{0:T(1024)(128)(2,1)S(1)}, bf16[2560]{0:T(1024)(128)(2,1)}, u32[]{:S(2)}) copy-start(bf16[2560]{0:T(1024)(128)(2,1)} %param.23) | copy-start | bytes 15364
  191.8 4.0 %copy-start.3 = (bf16[2560,16]{0,1:T(8,128)(2,1)S(1)}, bf16[2560,16]{0,1:T(8,128)(2,1)}, u32[]{:S(2)}) copy-start(bf16[2560,16]{0,1:T(8,128)(2,1)} %param.18) | copy-start | bytes 245764
  191.8 4.2 %copy-start.4 = (s32[64,6]{0,1:T(8,128)S(1)}, s32[64,6]{0,1:T(8,128)}, u32[]{:S(2)}) copy-start(s32[64,6]{0,1:T(8,128)} %param.19) | copy-start | bytes 4612
  191.8 120.6 %all-to-all-start.1 = ((bf16[32,32,2560]{2,1,0:T(8,128)(2,1)}), bf16[32,32,2560]{2,1,0:T(8,128)(2,1)}, u32[]{:S(2)}, u32[]{:S(2)}) async-start(bf16[32,32,2560]{2,1,0:T(8,128)(2,1)} %bitcast.74), calls=%async_computation.1 | async-start | bytes 10485760 | tf_op jit(solution)/shard_map/all_to_all | solution.py:94
  324.8 4.5 %copy-start.2 = (f32[64,2560]{1,0:T(8,128)S(1)}, f32[64,2560]{1,0:T(8,128)}, u32[]{:S(2)}) copy-start(f32[64,2560]{1,0:T(8,128)} %copy-done.1) | copy-start | bytes 1966084
  324.8 5.4 %copy-start.6 = (s32[1,64]{1,0:T(1,128)S(1)}, s32[1,64]{1,0:T(1,128)}, u32[]{:S(2)}) copy-start(s32[1,64]{1,0:T(1,128)} %param.16) | copy-start | bytes 772
where the time goes:
time: 331 us
  blocking collectives  162 us (49%)
  waiting for transfers between devices  116 us (35%)
  local copies, waits for them, and re-layouts  17.2 us (5%)
  matrix products  17 us (5%)
  other arithmetic  13.5 us (4%)
  starting transfers between devices  3.97 us (1%)
    all_to_all x1, blocking collectives, body(): lax.all_to_all(doubled.reshape(device_count, capacity, feature_count), 'e...  118 us
    all_to_all x1, waiting for transfers between devices, body(): lax.all_to_all(partials, 'expert', split_axis=0, concat_axis=0, tiled=True)  116 us
    all_gather x1, blocking collectives, body(): shard_rows = lax.all_gather(pooled, 'expert', axis=0, tiled=True)  44.1 us
  transfers between devices with their start and end apart: 1, of which 1 were waited for; matrix products, arithmetic and copies ran while one was open for 0% of the time, Pallas kernels for 0%

commit v1 on v0

v1 whole, which is shorter than its diff:
```python
import math

import jax
import jax.numpy as jnp
from jax import lax
from jax.sharding import PartitionSpec as P

epsilon = 1e-06


def expert_half(inputs, gate_rows, up_rows, down_rows):
    contract = (((1,), (1,)), ((), ()))
    gate_value = lax.dot_general(inputs, gate_rows, contract, preferred_element_type=jnp.float32)
    up_value = lax.dot_general(inputs, up_rows, contract, preferred_element_type=jnp.float32)
    active = (jax.nn.silu(gate_value) * up_value).astype(jnp.bfloat16)
    return jnp.dot(active, down_rows, preferred_element_type=jnp.float32)


def exchange(blocks):
    return lax.all_to_all(blocks, "expert", split_axis=0, concat_axis=0, tiled=True)


def body(
    text_rows,
    image_rows,
    image_probe,
    response_image,
    token_response,
    norm_gain,
    router_weight,
    expert_routes,
    gate_weight,
    up_weight,
    down_weight,
    reward_head,
):
    token_count, feature_count = text_rows.shape
    top_count = expert_routes.shape[1]
    expert_count = router_weight.shape[1]
    capacity = min(token_count, 4 * token_count * top_count // (3 * expert_count))
    device_count = lax.axis_size("expert")
    response_count = response_image.shape[0]
    probe_score = jnp.einsum(
        "ivd,d->iv", image_rows, image_probe, preferred_element_type=jnp.float32
    )
    pool_weight = jax.nn.sigmoid(probe_score).astype(jnp.bfloat16)
    pooled_sum = jnp.einsum(
        "iv,ivd->id", pool_weight, image_rows, preferred_element_type=jnp.float32
    )
    pooled = (pooled_sum / math.sqrt(image_rows.shape[1])).astype(jnp.bfloat16)
    copies = jnp.broadcast_to(pooled[None], (device_count,) + pooled.shape)
    shard_rows = exchange(copies).reshape(-1, feature_count)
    image_ids = jnp.arange(shard_rows.shape[0], dtype=jnp.int32)
    choose = (response_image[:, None] == image_ids[None, :]).astype(jnp.bfloat16)
    response_context = jnp.dot(choose, shard_rows, preferred_element_type=jnp.float32).astype(
        jnp.bfloat16
    )
    response_onehot = (
        token_response[0][:, None] == jnp.arange(response_count, dtype=jnp.int32)[None, :]
    )
    token_context = jnp.dot(
        response_onehot.astype(jnp.bfloat16), response_context, preferred_element_type=jnp.float32
    )
    hidden_state = text_rows.astype(jnp.float32) + token_context
    inverse = lax.rsqrt(jnp.mean(hidden_state * hidden_state, axis=-1, keepdims=True) + epsilon)
    normed = (hidden_state * inverse * norm_gain.astype(jnp.float32)).astype(jnp.bfloat16)
    logits = jnp.dot(normed, router_weight, preferred_element_type=jnp.float32)
    expert_ids = jnp.arange(expert_count, dtype=jnp.int32)
    member = jnp.any(expert_routes[:, :, None] == expert_ids[None, None, :], axis=1)
    chosen = jnp.where(member, jax.nn.sigmoid(logits), 0.0)
    route_weight = chosen / jnp.sum(chosen, axis=1, keepdims=True)
    positions = jnp.arange(token_count, dtype=jnp.int32)
    before = (positions[None, :] < positions[:, None]).astype(jnp.bfloat16)
    place = jnp.dot(before, member.astype(jnp.bfloat16), preferred_element_type=jnp.float32)
    slot_ids = jnp.arange(capacity, dtype=jnp.int32).astype(jnp.float32)
    taken = member[:, :, None] & (place[:, :, None] == slot_ids[None, None, :])
    slot_total = expert_count * capacity
    spread = taken.astype(jnp.bfloat16).reshape(token_count, slot_total)
    blend = jnp.where(taken, route_weight[:, :, None], 0.0).reshape(token_count, slot_total)
    outgoing = lax.dot_general(
        spread, normed, (((0,), (0,)), ((), ())), preferred_element_type=jnp.float32
    ).astype(jnp.bfloat16)
    share = slot_total // device_count
    swap = [(device, device ^ 1) for device in range(device_count)]
    weights = (gate_weight[0], up_weight[0], down_weight[0])
    mine = exchange(outgoing.reshape(device_count, share, feature_count))
    mine = mine.reshape(device_count * share, feature_count)
    other = lax.ppermute(mine, "expert", swap)
    own_part = expert_half(mine, *weights).astype(jnp.bfloat16)
    other_part = expert_half(other, *weights).astype(jnp.bfloat16)
    arrived_part = lax.ppermute(other_part, "expert", swap)
    summed = (own_part.astype(jnp.float32) + arrived_part.astype(jnp.float32)).astype(jnp.bfloat16)
    outputs = exchange(summed.reshape(device_count, share, feature_count))
    outputs = outputs.reshape(slot_total, feature_count)
    blend_high = blend.astype(jnp.bfloat16)
    blend_low = (blend - blend_high.astype(jnp.float32)).astype(jnp.bfloat16)
    mixture = jnp.dot(blend_high, outputs, preferred_element_type=jnp.float32)
    mixture = mixture + jnp.dot(blend_low, outputs, preferred_element_type=jnp.float32)
    combined = hidden_state + mixture
    reward = jnp.sum(combined * reward_head.astype(jnp.float32), axis=-1)
    totals = jnp.sum(jnp.where(response_onehot, reward[:, None], 0.0), axis=0)
    counts = jnp.sum(response_onehot.astype(jnp.float32), axis=0)
    return (combined.astype(jnp.bfloat16), totals / counts)


def solution(mesh):
    in_specs = (
        P(("group", "expert"), None),
        P(("group", "expert"), None, None),
        P(),
        P(("group", "expert")),
        P(("group", "expert"), None),
        P(),
        P(),
        P(("group", "expert"), None),
        P("expert", None, None),
        P("expert", None, None),
        P("expert", None, None),
        P(),
    )
    out_specs = (P(("group", "expert"), None), P(("group", "expert")))
    return jax.shard_map(body, mesh=mesh, in_specs=in_specs, out_specs=out_specs, check_vma=False)
```

time: 331 us -> 194 us (0.59)
  blocking collectives: 162 us -> 62.7 us
  waiting for transfers between devices: 116 us -> 70.4 us
  matrix products: 17 us -> 39.2 us
  local copies, waits for them, and re-layouts: 17.2 us -> 4.1 us
  other arithmetic: 13.5 us -> 5.64 us
  starting transfers between devices: 3.97 us -> 10.6 us
    all_to_all x1, blocking collectives: 118 us -> 62.7 us  [exchange(): lax.all_to_all(blocks, 'expert', split_axis=0, concat_axis=0, tiled=True)]
    all_to_all x1 -> x2, waiting for transfers between devices: 116 us -> 65.5 us  [exchange(): lax.all_to_all(blocks, 'expert', split_axis=0, concat_axis=0, tiled=True)]
    all_gather x1 -> x0, blocking collectives: 44.1 us -> none  [body(): shard_rows = lax.all_gather(pooled, 'expert', axis=0, tiled=True)]
    dot_general x1 -> x6, matrix products: 6.03 us -> 27.3 us  [the longest x2 23.3 us: expert_half(): return jnp.dot(active, down_rows, preferred_element_type=jnp.float32)]
    all_to_all x1 -> x2, starting transfers between devices: 3.97 us -> 10.4 us  [exchange(): lax.all_to_all(blocks, 'expert', split_axis=0, concat_axis=0, tiled=True)]
    gather x2 -> x0, local copies, waits for them, and re-layouts: 5.9 us -> none  [the longest x1 3.28 us: body(): outputs[places].reshape(token_count, top_count, feature_count)]
    reduce_sum x5 -> x0, other arithmetic: 5.58 us -> none  [the longest x1 4.51 us: body(): mixture = jnp.sum(route_weight[:, :, None] * gathered, axis=1)]
    ppermute x0 -> x2, waiting for transfers between devices: none -> 4.91 us  [the longest x1 4.91 us: body(): other = lax.ppermute(mine, 'expert', swap)]
  transfers between devices with their start and end apart: 1 -> 4, of which waited for: 1 -> 3; matrix products, arithmetic and copies ran while one was open for 0% -> 6% of each run, Pallas kernels for 0% -> 0%
where the time goes in v1:
time: 194 us; the launch traced here: 193 us
  waiting for transfers between devices  70.4 us (36%)
  blocking collectives  62.7 us (32%)
  matrix products  39.2 us (20%)
  starting transfers between devices  10.6 us (5%)
  other arithmetic  5.64 us (3%)
  local copies, waits for them, and re-layouts  4.1 us (2%)
    all_to_all x2, waiting for transfers between devices, exchange(): lax.all_to_all(blocks, 'expert', split_axis=0, concat_axis=0, tiled=True)  65.5 us
    all_to_all x1, blocking collectives, exchange(): lax.all_to_all(blocks, 'expert', split_axis=0, concat_axis=0, tiled=True)  62.7 us
    dot_general x2, matrix products, expert_half(): return jnp.dot(active, down_rows, preferred_element_type=jnp.float32)  23.3 us
    all_to_all x2, starting transfers between devices, exchange(): lax.all_to_all(blocks, 'expert', split_axis=0, concat_axis=0, tiled=True)  10.4 us
    dot_general x1, matrix products, expert_half(): lax.dot_general(inputs, gate_rows, contract, preferred_element_type=jnp.f...  5.54 us
    ppermute x1, waiting for transfers between devices, body(): other = lax.ppermute(mine, 'expert', swap)  4.91 us
  transfers between devices with their start and end apart: 4, of which 3 were waited for; matrix products, arithmetic and copies ran while one was open for 6% of the time, Pallas kernels for 0%

profile of v1, /device:TPU:0, one launch (start us, length us, event | category | flops | bytes accessed | tf_op | source)
XLA Modules:
  0.0 193.4 jit_solution(449800978773681571)
XLA Ops:
  0.6 0.7 reshape.128
  2.1 0.9 broadcast_in_dim.22
  3.0 7.3 %all-to-all-start = ((bf16[32,2,2560]{2,1,0:T(2,128)(2,1)}), bf16[32,2,2560]{2,1,0:T(2,128)(2,1)S(1)}, u32[]{:S(2)}, u32[]{:S(2)}) async-start(bf16[32,2,2560]{2,1,0:T(2,128)(2,1)} %broadcast_in_dim.22), calls=%async_computation | async-start | bytes 655360 | tf_op jit(solution)/shard_map/all_to_all | solution.py:20
  10.9 0.7 convert_element_type.111
  11.6 0.7 fusion.28
  12.6 9.7 %all-to-all-done = bf16[32,2,2560]{2,1,0:T(2,128)(2,1)S(1)} async-done(((bf16[32,2,2560]{2,1,0:T(2,128)(2,1)}), bf16[32,2,2560]{2,1,0:T(2,128)(2,1)S(1)}, u32[]{:S(2)}, u32[]{:S(2)}) %all-to-all-start) | async-done | bytes 327712 | tf_op jit(solution)/shard_map/all_to_all | solution.py:20
  22.4 1.5 multiply_reduce_fusion.1
  23.9 0.9 convolution_convert_fusion.2
  24.8 62.7 %all_to_all.15 = bf16[32,16,2560]{2,1,0:T(8,128)(2,1)S(1)} all-to-all(bf16[32,16,2560]{2,1,0:T(8,128)(2,1)S(1)} %bitcast.63), channel_id=1, replica_groups=mesh['group'=1,'expert'=32] {'expert'}, dimensions={0} | all-to-all | bytes 5242880 | tf_op jit(solution)/shard_map/all_to_all | solution.py:20
  87.6 4.9 %collective-permute-done = bf16[512,2560]{1,0:T(8,128)(2,1)S(1)} collective-permute-done((bf16[512,2560]{1,0:T(8,128)(2,1)S(1)}, bf16[512,2560]{1,0:T(8,128)(2,1)S(1)}, u32[]{:S(2)}, u32[]{:S(2)}) %collective-permute-start) | collective-permute-done | bytes 2621472 | tf_op jit(solution)/shard_map/ppermute | solution.py:88
  92.5 1.5 copy-done.9
  94.0 3.4 %fusion.2 = f32[512,768]{1,0:T(8,128)} fusion(bf16[512,2560]{1,0:T(8,128)(2,1)S(1)} %collective-permute-done, bf16[1,768,2560]{2,1,0:T(8,128)(2,1)S(1)} %copy-done.8), kind=kOutput, calls=%fused_computation.6 | convolution fusion | flops 2013265920 | bytes 8126464 | tf_op jit(solution)/shard_map/dot_general | solution.py:14
  97.4 11.6 %convolution_convert_fusion = bf16[512,2560]{1,0:T(8,128)(2,1)} fusion(bf16[1,768,2560]{2,1,0:T(8,128)(2,1)} %param.22, f32[512,768]{1,0:T(8,128)} %fusion.2, bf16[512,2560]{1,0:T(8,128)(2,1)} %copy-done.9, bf16[1,768,2560]{2,1,0:T(8,128)(2,1)} %param.20), kind=kOutput, calls=%fused_computation.1 | convolution fusion | flops 4030201856 | bytes 14680064 | tf_op jit(solution)/shard_map/dot_general | solution.py:16
  109.2 5.5 %fusion.8 = f32[512,768]{1,0:T(8,128)} fusion(bf16[512,2560]{1,0:T(8,128)(2,1)S(1)} %bitcast.66, bf16[1,768,2560]{2,1,0:T(8,128)(2,1)} %param.20), kind=kOutput, calls=%fused_computation.12 | convolution fusion | flops 2013265920 | bytes 8126464 | tf_op jit(solution)/shard_map/dot_general | solution.py:13
  114.8 11.6 %add_convert_fusion = bf16[512,2560]{1,0:T(8,128)(2,1)} fusion(bf16[512,2560]{1,0:T(8,128)(2,1)} %collective-permute-done.1, bf16[1,768,2560]{2,1,0:T(8,128)(2,1)} %param.22, f32[512,768]{1,0:T(8,128)} %fusion.8, bf16[512,2560]{1,0:T(8,128)(2,1)S(1)} %bitcast.67, bf16[1,768,2560]{2,1,0:T(8,128)(2,1)} %param.21), kind=kOutput, calls=%fused_computation | convolution fusion | flops 4035444736 | bytes 17301504 | tf_op jit(solution)/shard_map/dot_general | solution.py:16
  126.4 3.1 %all-to-all-start.2 = ((bf16[32,16,2560]{2,1,0:T(8,128)(2,1)}), bf16[32,16,2560]{2,1,0:T(8,128)(2,1)S(1)}, u32[]{:S(2)}, u32[]{:S(2)}) async-start(bf16[32,16,2560]{2,1,0:T(8,128)(2,1)} %bitcast.64), calls=%async_computation.2 | async-start | bytes 5242880 | tf_op jit(solution)/shard_map/all_to_all | solution.py:20
  129.5 0.6 convert_element_type.127
  130.1 0.9 fusion.40
  131.1 1.4 select_convert_fusion
  132.5 1.4 fusion.26
  133.9 55.8 %all-to-all-done.2 = bf16[32,16,2560]{2,1,0:T(8,128)(2,1)S(1)} async-done(((bf16[32,16,2560]{2,1,0:T(8,128)(2,1)}), bf16[32,16,2560]{2,1,0:T(8,128)(2,1)S(1)}, u32[]{:S(2)}, u32[]{:S(2)}) %all-to-all-start.2) | async-done | bytes 2621472 | tf_op jit(solution)/shard_map/all_to_all | solution.py:20
  189.7 1.5 fusion.42
  191.3 1.5 multiply_reduce_fusion
  192.9 0.5 div.46
  (35 shorter events, 2.0 us)
Async XLA Ops:
  0.6 0.9 copy-start
  3.0 19.3 %all-to-all-start = ((bf16[32,2,2560]{2,1,0:T(2,128)(2,1)}), bf16[32,2,2560]{2,1,0:T(2,128)(2,1)S(1)}, u32[]{:S(2)}, u32[]{:S(2)}) async-start(bf16[32,2,2560]{2,1,0:T(2,128)(2,1)} %broadcast_in_dim.22), calls=%async_computation | async-start | bytes 655360 | tf_op jit(solution)/shard_map/all_to_all | solution.py:20
  10.3 0.5 copy-start.5
  23.9 63.6 %copy-start.7 = (f32[64]{0:T(128)}, f32[64]{0:T(128)S(1)}, u32[]{:S(2)}) copy-start(f32[64]{0:T(128)S(1)} %add_rsqrt_fusion) | copy-start | bytes 772
  24.8 69.2 %copy-start.8 = (bf16[1,768,2560]{2,1,0:T(8,128)(2,1)S(1)}, bf16[1,768,2560]{2,1,0:T(8,128)(2,1)}, u32[]{:S(2)}) copy-start(bf16[1,768,2560]{2,1,0:T(8,128)(2,1)} %param.21) | copy-start | bytes 11796484
  87.6 4.9 %collective-permute-start = (bf16[512,2560]{1,0:T(8,128)(2,1)S(1)}, bf16[512,2560]{1,0:T(8,128)(2,1)S(1)}, u32[]{:S(2)}, u32[]{:S(2)}) collective-permute-start(bf16[512,2560]{1,0:T(8,128)(2,1)S(1)} %bitcast.65), channel_id=1, source_target_pairs={{0,1},{1,0},{2,3},{3,2},{4,5},{5,4},{6,7},{7,6},{8,9},{9,8},{10,11... | collective-permute-start | bytes 7864328 | tf_op jit(solution)/shard_map/ppermute | solution.py:88
  92.5 1.5 copy-start.9
  109.1 5.7 %collective-permute-start.1 = (bf16[512,2560]{1,0:T(8,128)(2,1)}, bf16[512,2560]{1,0:T(8,128)(2,1)}, u32[]{:S(2)}, u32[]{:S(2)}) collective-permute-start(bf16[512,2560]{1,0:T(8,128)(2,1)} %convolution_convert_fusion), channel_id=1, source_target_pairs={{0,1},{1,0},{2,3},{3,2},{4,5},{5,4},{6,7},{7,6},{8,9},{9,8},{10,11... | collective-permute-start | bytes 7864328 | tf_op jit(solution)/shard_map/ppermute | solution.py:91
  126.4 3.1 %copy-start.4 = (bf16[2560]{0:T(1024)(128)(2,1)S(1)}, bf16[2560]{0:T(1024)(128)(2,1)}, u32[]{:S(2)}) copy-start(bf16[2560]{0:T(1024)(128)(2,1)} %param.23) | copy-start | bytes 15364
  126.4 3.8 %copy-start.2 = (bf16[2560,16]{0,1:T(8,128)(2,1)S(1)}, bf16[2560,16]{0,1:T(8,128)(2,1)}, u32[]{:S(2)}) copy-start(bf16[2560,16]{0,1:T(8,128)(2,1)} %param.18) | copy-start | bytes 245764
  126.4 63.3 %all-to-all-start.2 = ((bf16[32,16,2560]{2,1,0:T(8,128)(2,1)}), bf16[32,16,2560]{2,1,0:T(8,128)(2,1)S(1)}, u32[]{:S(2)}, u32[]{:S(2)}) async-start(bf16[32,16,2560]{2,1,0:T(8,128)(2,1)} %bitcast.64), calls=%async_computation.2 | async-start | bytes 5242880 | tf_op jit(solution)/shard_map/all_to_all | solution.py:20
  131.1 60.1 %copy-start.3 = (f32[2560]{0:T(1024)S(1)}, f32[2560]{0:T(1024)}, u32[]{:S(2)}) copy-start(f32[2560]{0:T(1024)} %convert_element_type.127) | copy-start | bytes 30724
  189.7 1.6 copy-start.1
  191.2 1.5 copy-start.6

commit v2 on v1

--- a/solution.py
+++ b/solution.py
@@ -13,11 +13,62 @@
     gate_value = lax.dot_general(inputs, gate_rows, contract, preferred_element_type=jnp.float32)
     up_value = lax.dot_general(inputs, up_rows, contract, preferred_element_type=jnp.float32)
     active = (jax.nn.silu(gate_value) * up_value).astype(jnp.bfloat16)
+    active = lax.optimization_barrier(active)
     return jnp.dot(active, down_rows, preferred_element_type=jnp.float32)
 
 
-def exchange(blocks):
-    return lax.all_to_all(blocks, "expert", split_axis=0, concat_axis=0, tiled=True)
+def exchange(blocks, groups=None):
+    return lax.all_to_all(
+        blocks, "expert", split_axis=0, concat_axis=0, axis_index_groups=groups, tiled=True
+    )
+
+
+def slot_onehot(routes, first_expert, side_experts, capacity):
+    token_count = routes.shape[0]
+    expert_ids = first_expert + jnp.arange(side_experts, dtype=jnp.int32)
+    member = jnp.any(routes[:, :, None] == expert_ids[None, None, :], axis=1)
+    positions = jnp.arange(token_count, dtype=jnp.int32)
+    before = (positions[None, :] < positions[:, None]).astype(jnp.bfloat16)
+    place = jnp.dot(before, member.astype(jnp.bfloat16), preferred_element_type=jnp.float32)
+    slot_ids = jnp.arange(capacity, dtype=jnp.int32).astype(jnp.float32)
+    return member[:, :, None] & (place[:, :, None] == slot_ids[None, None, :])
+
+
+def slot_blend(taken, normed, routes, router_weight, first_expert):
+    token_count, side_experts, capacity = taken.shape
+    logits = jnp.dot(normed, router_weight, preferred_element_type=jnp.float32)
+    expert_ids = jnp.arange(router_weight.shape[1], dtype=jnp.int32)
+    member = jnp.any(routes[:, :, None] == expert_ids[None, None, :], axis=1)
+    chosen = jnp.where(member, jax.nn.sigmoid(logits), 0.0)
+    route_weight = chosen / jnp.sum(chosen, axis=1, keepdims=True)
+    route_weight = lax.dynamic_slice_in_dim(route_weight, first_expert, side_experts, axis=1)
+    high = route_weight.astype(jnp.bfloat16)
+    low = (route_weight - high.astype(jnp.float32)).astype(jnp.bfloat16)
+    zero = jnp.zeros((), jnp.bfloat16)
+    flat = (token_count, side_experts * capacity)
+    return tuple(jnp.where(taken, part[:, :, None], zero).reshape(flat) for part in (high, low))
+
+
+def fill_slots(taken, normed):
+    spread = taken.astype(jnp.bfloat16).reshape(taken.shape[0], -1)
+    return lax.dot_general(
+        spread, normed, (((0,), (0,)), ((), ())), preferred_element_type=jnp.float32
+    ).astype(jnp.bfloat16)
+
+
+def run_expert(mine, swap, weights):
+    rows = mine.shape[0]
+    other = lax.ppermute(mine, "expert", swap)
+    parts = expert_half(jnp.concatenate([mine, other], axis=0), *weights).astype(jnp.bfloat16)
+    arrived = lax.ppermute(parts[rows:], "expert", swap)
+    return (parts[:rows].astype(jnp.float32) + arrived.astype(jnp.float32)).astype(jnp.bfloat16)
+
+
+def mix(blend, outputs):
+    high, low = blend
+    return jnp.dot(high, outputs, preferred_element_type=jnp.float32) + jnp.dot(
+        low, outputs, preferred_element_type=jnp.float32
+    )
 
 
 def body(
@@ -64,38 +115,31 @@
     hidden_state = text_rows.astype(jnp.float32) + token_context
     inverse = lax.rsqrt(jnp.mean(hidden_state * hidden_state, axis=-1, keepdims=True) + epsilon)
     normed = (hidden_state * inverse * norm_gain.astype(jnp.float32)).astype(jnp.bfloat16)
-    logits = jnp.dot(normed, router_weight, preferred_element_type=jnp.float32)
-    expert_ids = jnp.arange(expert_count, dtype=jnp.int32)
-    member = jnp.any(expert_routes[:, :, None] == expert_ids[None, None, :], axis=1)
-    chosen = jnp.where(member, jax.nn.sigmoid(logits), 0.0)
-    route_weight = chosen / jnp.sum(chosen, axis=1, keepdims=True)
-    positions = jnp.arange(token_count, dtype=jnp.int32)
-    before = (positions[None, :] < positions[:, None]).astype(jnp.bfloat16)
-    place = jnp.dot(before, member.astype(jnp.bfloat16), preferred_element_type=jnp.float32)
-    slot_ids = jnp.arange(capacity, dtype=jnp.int32).astype(jnp.float32)
-    taken = member[:, :, None] & (place[:, :, None] == slot_ids[None, None, :])
-    slot_total = expert_count * capacity
-    spread = taken.astype(jnp.bfloat16).reshape(token_count, slot_total)
-    blend = jnp.where(taken, route_weight[:, :, None], 0.0).reshape(token_count, slot_total)
-    outgoing = lax.dot_general(
-        spread, normed, (((0,), (0,)), ((), ())), preferred_element_type=jnp.float32
-    ).astype(jnp.bfloat16)
-    share = slot_total // device_count
+    side_experts = expert_count // 2
+    half = device_count // 2
+    first_expert = (lax.axis_index("expert") // half) * side_experts
+    across = [(device, (device + half) % device_count) for device in range(device_count)]
+    sides = [list(range(half)), list(range(half, device_count))]
     swap = [(device, device ^ 1) for device in range(device_count)]
     weights = (gate_weight[0], up_weight[0], down_weight[0])
-    mine = exchange(outgoing.reshape(device_count, share, feature_count))
-    mine = mine.reshape(device_count * share, feature_count)
-    other = lax.ppermute(mine, "expert", swap)
-    own_part = expert_half(mine, *weights).astype(jnp.bfloat16)
-    other_part = expert_half(other, *weights).astype(jnp.bfloat16)
-    arrived_part = lax.ppermute(other_part, "expert", swap)
-    summed = (own_part.astype(jnp.float32) + arrived_part.astype(jnp.float32)).astype(jnp.bfloat16)
-    outputs = exchange(summed.reshape(device_count, share, feature_count))
-    outputs = outputs.reshape(slot_total, feature_count)
-    blend_high = blend.astype(jnp.bfloat16)
-    blend_low = (blend - blend_high.astype(jnp.float32)).astype(jnp.bfloat16)
-    mixture = jnp.dot(blend_high, outputs, preferred_element_type=jnp.float32)
-    mixture = mixture + jnp.dot(blend_low, outputs, preferred_element_type=jnp.float32)
+    far_routes = lax.ppermute(expert_routes, "expert", across)
+    far_normed = lax.ppermute(normed, "expert", across)
+    near_taken = slot_onehot(expert_routes, first_expert, side_experts, capacity)
+    far_taken = slot_onehot(far_routes, first_expert, side_experts, capacity)
+    slot_total = side_experts * capacity
+    blocks = (half, slot_total // half, feature_count)
+    flat = (slot_total, feature_count)
+    near_in = exchange(fill_slots(near_taken, normed).reshape(blocks), sides).reshape(flat)
+    far_in = exchange(fill_slots(far_taken, far_normed).reshape(blocks), sides).reshape(flat)
+    near_sum = run_expert(near_in, swap, weights)
+    far_sum = run_expert(far_in, swap, weights)
+    near_sum, far_sum = lax.optimization_barrier((near_sum, far_sum))
+    far_out = exchange(far_sum.reshape(blocks), sides).reshape(flat)
+    near_out = exchange(near_sum.reshape(blocks), sides).reshape(flat)
+    far_blend = slot_blend(far_taken, far_normed, far_routes, router_weight, first_expert)
+    near_blend = slot_blend(near_taken, normed, expert_routes, router_weight, first_expert)
+    far_mixture = lax.ppermute(mix(far_blend, far_out).astype(jnp.bfloat16), "expert", across)
+    mixture = mix(near_blend, near_out) + far_mixture.astype(jnp.float32)
     combined = hidden_state + mixture
     reward = jnp.sum(combined * reward_head.astype(jnp.float32), axis=-1)
     totals = jnp.sum(jnp.where(response_onehot, reward[:, None], 0.0), axis=0)

time: 194 us -> 161 us (0.83)
  blocking collectives: 62.7 us -> 22.5 us
  starting transfers between devices: 10.6 us -> 26.5 us
  matrix products: 39.2 us -> 30.8 us
    all_to_all x1, blocking collectives: 62.7 us -> 22.5 us  [exchange(): lax.all_to_all(blocks, 'expert', split_axis=0, concat_axis=0, axis_index_...]
    ppermute x2 -> x7, waiting for transfers between devices: 4.91 us -> 29.9 us  [the longest x1 20.8 us: body(): far_normed = lax.ppermute(normed, 'expert', across)]
    all_to_all x2 -> x4, waiting for transfers between devices: 65.5 us -> 41.4 us  [exchange(): lax.all_to_all(blocks, 'expert', split_axis=0, concat_axis=0, axis_index_...]
    dot_general x2, matrix products: 23.3 us -> 4.4 us  [expert_half(): return jnp.dot(active, down_rows, preferred_element_type=jnp.float32)]
    all_to_all x2 -> x4, starting transfers between devices: 10.4 us -> 20.3 us  [exchange(): lax.all_to_all(blocks, 'expert', split_axis=0, concat_axis=0, axis_index_...]
    ppermute x2 -> x7, starting transfers between devices: 0.15 us -> 6.16 us  [the longest x1 2.74 us: body(): far_routes = lax.ppermute(expert_routes, 'expert', across)]
    dot_general x5 -> x10, matrix products: 4.95 us -> 9.64 us  [the longest x2 3.11 us: fill_slots(): lax.dot_general(spread, normed, (((0,), (0,)), ((), ())), preferred_eleme...]
    dot_general x1 -> x2, matrix products: 3.43 us -> 7.41 us  [expert_half(): lax.dot_general(inputs, up_rows, contract, preferred_element_type=jnp.flo...]
  transfers between devices with their start and end apart: 4 -> 11, of which waited for: 3 -> 6; matrix products, arithmetic and copies ran while one was open for 6% -> 19% of each run, Pallas kernels for 0% -> 0%
where the time goes in v2:
time: 161 us; the launch traced here: 160 us
  waiting for transfers between devices  71.2 us (44%)
  matrix products  30.8 us (19%)
  starting transfers between devices  26.5 us (16%)
  blocking collectives  22.5 us (14%)
  other arithmetic  4.99 us (3%)
  local copies, waits for them, and re-layouts  2.93 us (2%)
    all_to_all x4, waiting for transfers between devices, exchange(): lax.all_to_all(blocks, 'expert', split_axis=0, concat_axis=0, axis_index_...  41.4 us
    all_to_all x1, blocking collectives, exchange(): lax.all_to_all(blocks, 'expert', split_axis=0, concat_axis=0, axis_index_...  22.5 us
    ppermute x1, waiting for transfers between devices, body(): far_normed = lax.ppermute(normed, 'expert', across)  20.8 us
    all_to_all x4, starting transfers between devices, exchange(): lax.all_to_all(blocks, 'expert', split_axis=0, concat_axis=0, axis_index_...  20.3 us
    dot_general x2, matrix products, expert_half(): lax.dot_general(inputs, gate_rows, contract, preferred_element_type=jnp.f...  8.41 us
    ppermute x1, waiting for transfers between devices, body(): far_routes = lax.ppermute(expert_routes, 'expert', across)  7.44 us
    dot_general x2, matrix products, expert_half(): lax.dot_general(inputs, up_rows, contract, preferred_element_type=jnp.flo...  7.41 us
    dot_general x2, matrix products, expert_half(): return jnp.dot(active, down_rows, preferred_element_type=jnp.float32)  4.4 us
  transfers between devices with their start and end apart: 11, of which 6 were waited for; matrix products, arithmetic and copies ran while one was open for 19% of the time, Pallas kernels for 0%

profile of v2, /device:TPU:0, one launch (start us, length us, event | category | flops | bytes accessed | tf_op | source)
XLA Modules:
  0.0 159.9 jit_solution(8496149915661102364)
XLA Ops:
  2.9 7.3 %all-to-all-start = ((bf16[32,2,2560]{2,1,0:T(2,128)(2,1)}), bf16[32,2,2560]{2,1,0:T(2,128)(2,1)S(1)}, u32[]{:S(2)}, u32[]{:S(2)}) async-start(bf16[32,2,2560]{2,1,0:T(2,128)(2,1)} %broadcast_in_dim.45), calls=%async_computation | async-start | bytes 655360 | tf_op jit(solution)/shard_map/all_to_all | solution.py:21
  10.2 2.7 %collective-permute-start.2 = (s32[64,6]{0,1:T(8,128)}, s32[64,6]{0,1:T(8,128)S(1)}, u32[]{:S(2)}, u32[]{:S(2)}) collective-permute-start(s32[64,6]{0,1:T(8,128)} %param.19), channel_id=1, source_target_pairs={{0,16},{1,17},{2,18},{3,19},{4,20},{5,21},{6,22},{7,23},{8,24},{9,... | collective-permute-start | bytes 4616 | tf_op jit(solution)/shard_map/ppermute | solution.py:125
  13.8 7.4 %collective-permute-done.2 = s32[64,6]{0,1:T(8,128)S(1)} collective-permute-done((s32[64,6]{0,1:T(8,128)}, s32[64,6]{0,1:T(8,128)S(1)}, u32[]{:S(2)}, u32[]{:S(2)}) %collective-permute-start.2) | collective-permute-done | bytes 1568 | tf_op jit(solution)/shard_map/ppermute | solution.py:125
  23.2 1.6 convolution_convert_fusion.3
  24.8 3.8 %all-to-all-start.1 = ((bf16[16,16,2560]{2,1,0:T(8,128)(2,1)}), bf16[16,16,2560]{2,1,0:T(8,128)(2,1)S(1)}, u32[]{:S(2)}, u32[]{:S(2)}) async-start(bf16[16,16,2560]{2,1,0:T(8,128)(2,1)} %bitcast.8), calls=%async_computation.1 | async-start | bytes 2621440 | tf_op jit(solution)/shard_map/all_to_all | solution.py:21
  28.6 1.5 collective-permute-start.3
  30.1 20.8 %collective-permute-done.3 = bf16[64,2560]{1,0:T(8,128)(2,1)S(1)} collective-permute-done((bf16[64,2560]{1,0:T(8,128)(2,1)S(1)}, bf16[64,2560]{1,0:T(8,128)(2,1)S(1)}, u32[]{:S(2)}, u32[]{:S(2)}) %collective-permute-start.3) | collective-permute-done | bytes 327712 | tf_op jit(solution)/shard_map/ppermute | solution.py:126
  51.6 1.6 convolution_convert_fusion.2
  53.2 1.5 all-to-all-done.1
  54.6 5.4 %all-to-all-start.2 = ((bf16[16,16,2560]{2,1,0:T(8,128)(2,1)}), bf16[16,16,2560]{2,1,0:T(8,128)(2,1)}, u32[]{:S(2)}, u32[]{:S(2)}) async-start(bf16[16,16,2560]{2,1,0:T(8,128)(2,1)} %bitcast.15), calls=%async_computation.2 | async-start | bytes 2621440 | tf_op jit(solution)/shard_map/all_to_all | solution.py:21
  60.4 19.0 %all-to-all-done.2 = bf16[16,16,2560]{2,1,0:T(8,128)(2,1)} async-done(((bf16[16,16,2560]{2,1,0:T(8,128)(2,1)}), bf16[16,16,2560]{2,1,0:T(8,128)(2,1)}, u32[]{:S(2)}, u32[]{:S(2)}) %all-to-all-start.2) | async-done | bytes 1310752 | tf_op jit(solution)/shard_map/all_to_all | solution.py:21
  79.5 4.9 %fusion.8 = f32[512,768]{1,0:T(8,128)S(1)} fusion(bf16[1,768,2560]{2,1,0:T(8,128)(2,1)} %param.20, bf16[256,2560]{1,0:T(8,128)(2,1)} %collective-permute-done, bf16[256,2560]{1,0:T(8,128)(2,1)S(1)} %bitcast.83), kind=kOutput, calls=%fused_computation.10 | convolution fusion | flops 2018508800 | bytes 8126464 | tf_op jit(solution)/shard_map/dot_general | solution.py:13
  84.4 3.8 %multiply_convert_fusion.1 = bf16[512,768]{1,0:T(8,128)(2,1)S(1)} fusion(f32[512,768]{1,0:T(8,128)S(1)} %fusion.8, bf16[1,768,2560]{2,1,0:T(8,128)(2,1)S(1)} %copy-done.10, bf16[256,2560]{1,0:T(8,128)(2,1)} %collective-permute-done, bf16[256,2560]{1,0:T(8,128)(2,1)S(1)} %bitcast.84), kind=kOutput, calls=%fused_computation.24 | convolution fusion | flops 2020868096 | bytes 8912896 | tf_op jit(solution)/shard_map/dot_general | solution.py:14
  88.2 2.2 %convolution_convert_fusion.1 = bf16[512,2560]{1,0:T(8,128)(2,1)S(1)} fusion(bf16[512,768]{1,0:T(8,128)(2,1)S(1)} %multiply_convert_fusion.1, bf16[1,768,2560]{2,1,0:T(8,128)(2,1)S(1)} %copy-done.11), kind=kOutput, calls=%fused_computation.1 | convolution fusion | flops 2014576640 | bytes 7340032 | tf_op jit(solution)/shard_map/dot_general | solution.py:17
  91.2 3.5 %fusion.6 = f32[512,768]{1,0:T(8,128)S(1)} fusion(bf16[1,768,2560]{2,1,0:T(8,128)(2,1)S(1)} %copy-done.9, bf16[256,2560]{1,0:T(8,128)(2,1)S(1)} %collective-permute-done.4, bf16[256,2560]{1,0:T(8,128)(2,1)} %bitcast.16), kind=kOutput, calls=%fused_computation.8 | convolution fusion | flops 2018508800 | bytes 8126464 | tf_op jit(solution)/shard_map/dot_general | solution.py:13
  94.8 3.6 %multiply_convert_fusion = bf16[512,768]{1,0:T(8,128)(2,1)S(1)} fusion(f32[512,768]{1,0:T(8,128)S(1)} %fusion.6, bf16[1,768,2560]{2,1,0:T(8,128)(2,1)S(1)} %copy-done.10, bf16[256,2560]{1,0:T(8,128)(2,1)S(1)} %collective-permute-done.4, bf16[256,2560]{1,0:T(8,128)(2,1)} %bitcast.16), kind=kOutput, calls=%fused_computation.23 | convolution fusion | flops 2020868096 | bytes 8912896 | tf_op jit(solution)/shard_map/dot_general | solution.py:14
  98.4 2.2 %convolution_convert_fusion = bf16[512,2560]{1,0:T(8,128)(2,1)S(1)} fusion(bf16[512,768]{1,0:T(8,128)(2,1)S(1)} %multiply_convert_fusion, bf16[1,768,2560]{2,1,0:T(8,128)(2,1)S(1)} %copy-done.11), kind=kOutput, calls=%fused_computation | convolution fusion | flops 2014576640 | bytes 7340032 | tf_op jit(solution)/shard_map/dot_general | solution.py:17
  100.8 1.4 add_convert_fusion.1
  102.2 1.6 %collective-permute-done.5 = bf16[256,2560]{1,0:T(8,128)(2,1)S(1)} collective-permute-done((bf16[256,2560]{1,0:T(8,128)(2,1)S(1)}, bf16[256,2560]{1,0:T(8,128)(2,1)S(1)}, u32[]{:S(2)}, u32[]{:S(2)}) %collective-permute-start.5) | collective-permute-done | bytes 1310752 | tf_op jit(solution)/shard_map/ppermute | solution.py:63
  104.1 22.5 %all_to_all.25 = bf16[16,16,2560]{2,1,0:T(8,128)(2,1)S(1)} all-to-all(bf16[16,16,2560]{2,1,0:T(8,128)(2,1)S(1)} %bitcast.81), channel_id=1, replica_groups={{0,1,2,3,4,5,6,7,8,9,10,11,12,13,14,15},{16,17,18,19,20,21,22,23,24,25,..., dimensions={0} | all-to-all | bytes 2621440 | tf_op jit(solution)/shard_map/all_to_all | solution.py:21
  126.7 3.8 %all-to-all-start.3 = ((bf16[16,16,2560]{2,1,0:T(8,128)(2,1)}), bf16[16,16,2560]{2,1,0:T(8,128)(2,1)S(1)}, u32[]{:S(2)}, u32[]{:S(2)}) async-start(bf16[16,16,2560]{2,1,0:T(8,128)(2,1)} %bitcast.80), calls=%async_computation.3 | async-start | bytes 2621440 | tf_op jit(solution)/shard_map/all_to_all | solution.py:21
  136.0 20.8 %all-to-all-done.3 = bf16[16,16,2560]{2,1,0:T(8,128)(2,1)S(1)} async-done(((bf16[16,16,2560]{2,1,0:T(8,128)(2,1)}), bf16[16,16,2560]{2,1,0:T(8,128)(2,1)S(1)}, u32[]{:S(2)}, u32[]{:S(2)}) %all-to-all-start.3) | async-done | bytes 1310752 | tf_op jit(solution)/shard_map/all_to_all | solution.py:21
  156.8 1.2 fusion.53
  158.0 1.2 multiply_reduce_fusion
  (68 shorter events, 13.5 us)
Async XLA Ops:
  0.6 0.9 copy-start
  0.6 21.9 %copy-start.8 = (s32[4]{0:T(128)S(1)}, s32[4]{0:T(128)}, u32[]{:S(2)}) copy-start(s32[4]{0:T(128)} %param.15) | copy-start | bytes 52
  0.7 21.9 %copy-start.7 = (s32[1,64]{1,0:T(1,128)S(1)}, s32[1,64]{1,0:T(1,128)}, u32[]{:S(2)}) copy-start(s32[1,64]{1,0:T(1,128)} %param.16) | copy-start | bytes 772
  0.7 21.9 %copy-start.4 = (bf16[64,2560]{1,0:T(8,128)(2,1)S(1)}, bf16[64,2560]{1,0:T(8,128)(2,1)}, u32[]{:S(2)}) copy-start(bf16[64,2560]{1,0:T(8,128)(2,1)} %param.12) | copy-start | bytes 983044
  2.9 19.4 %all-to-all-start = ((bf16[32,2,2560]{2,1,0:T(2,128)(2,1)}), bf16[32,2,2560]{2,1,0:T(2,128)(2,1)S(1)}, u32[]{:S(2)}, u32[]{:S(2)}) async-start(bf16[32,2,2560]{2,1,0:T(2,128)(2,1)} %broadcast_in_dim.45), calls=%async_computation | async-start | bytes 655360 | tf_op jit(solution)/shard_map/all_to_all | solution.py:21
  10.2 11.0 %collective-permute-start.2 = (s32[64,6]{0,1:T(8,128)}, s32[64,6]{0,1:T(8,128)S(1)}, u32[]{:S(2)}, u32[]{:S(2)}) collective-permute-start(s32[64,6]{0,1:T(8,128)} %param.19), channel_id=1, source_target_pairs={{0,16},{1,17},{2,18},{3,19},{4,20},{5,21},{6,22},{7,23},{8,24},{9,... | collective-permute-start | bytes 4616 | tf_op jit(solution)/shard_map/ppermute | solution.py:125
  23.2 5.4 %copy-start.1 = (bf16[64,2560]{1,0:T(8,128)(2,1)}, bf16[64,2560]{1,0:T(8,128)(2,1)S(1)}, u32[]{:S(2)}) copy-start(bf16[64,2560]{1,0:T(8,128)(2,1)S(1)} %multiply_convert_fusion.2) | copy-start | bytes 983044
  24.8 29.8 %all-to-all-start.1 = ((bf16[16,16,2560]{2,1,0:T(8,128)(2,1)}), bf16[16,16,2560]{2,1,0:T(8,128)(2,1)S(1)}, u32[]{:S(2)}, u32[]{:S(2)}) async-start(bf16[16,16,2560]{2,1,0:T(8,128)(2,1)} %bitcast.8), calls=%async_computation.1 | async-start | bytes 2621440 | tf_op jit(solution)/shard_map/all_to_all | solution.py:21
  28.6 22.3 %collective-permute-start.3 = (bf16[64,2560]{1,0:T(8,128)(2,1)S(1)}, bf16[64,2560]{1,0:T(8,128)(2,1)S(1)}, u32[]{:S(2)}, u32[]{:S(2)}) collective-permute-start(bf16[64,2560]{1,0:T(8,128)(2,1)S(1)} %multiply_convert_fusion.2), channel_id=1, source_target_pairs={{0,16},{1,17},{2,18},{3,19},{4,20},{5,21},{6,22},{7,23},{8,24},{9,... | collective-permute-start | bytes 983048 | tf_op jit(solution)/shard_map/ppermute | solution.py:126
  50.9 0.7 copy-start.2
  54.6 24.8 %all-to-all-start.2 = ((bf16[16,16,2560]{2,1,0:T(8,128)(2,1)}), bf16[16,16,2560]{2,1,0:T(8,128)(2,1)}, u32[]{:S(2)}, u32[]{:S(2)}) async-start(bf16[16,16,2560]{2,1,0:T(8,128)(2,1)} %bitcast.15), calls=%async_computation.2 | async-start | bytes 2621440 | tf_op jit(solution)/shard_map/all_to_all | solution.py:21
  60.1 19.4 %collective-permute-start = (bf16[256,2560]{1,0:T(8,128)(2,1)S(1)}, bf16[256,2560]{1,0:T(8,128)(2,1)}, u32[]{:S(2)}, u32[]{:S(2)}) collective-permute-start(bf16[256,2560]{1,0:T(8,128)(2,1)S(1)} %bitcast.82), channel_id=1, source_target_pairs={{0,1},{1,0},{2,3},{3,2},{4,5},{5,4},{6,7},{7,6},{8,9},{9,8},{10,11... | collective-permute-start | bytes 3932168 | tf_op jit(solution)/shard_map/ppermute | solution.py:61
  79.5 4.9 %copy-start.10 = (bf16[1,768,2560]{2,1,0:T(8,128)(2,1)S(1)}, bf16[1,768,2560]{2,1,0:T(8,128)(2,1)}, u32[]{:S(2)}) copy-start(bf16[1,768,2560]{2,1,0:T(8,128)(2,1)} %param.21) | copy-start | bytes 11796484
  79.5 11.7 %collective-permute-start.4 = (bf16[256,2560]{1,0:T(8,128)(2,1)}, bf16[256,2560]{1,0:T(8,128)(2,1)S(1)}, u32[]{:S(2)}, u32[]{:S(2)}) collective-permute-start(bf16[256,2560]{1,0:T(8,128)(2,1)} %bitcast.16), channel_id=1, source_target_pairs={{0,1},{1,0},{2,3},{3,2},{4,5},{5,4},{6,7},{7,6},{8,9},{9,8},{10,11... | collective-permute-start | bytes 3932168 | tf_op jit(solution)/shard_map/ppermute | solution.py:61
  84.4 3.8 %copy-start.11 = (bf16[1,768,2560]{2,1,0:T(8,128)(2,1)S(1)}, bf16[1,768,2560]{2,1,0:T(8,128)(2,1)}, u32[]{:S(2)}) copy-start(bf16[1,768,2560]{2,1,0:T(8,128)(2,1)} %param.22) | copy-start | bytes 11796484
  88.2 3.0 %copy-start.9 = (bf16[1,768,2560]{2,1,0:T(8,128)(2,1)S(1)}, bf16[1,768,2560]{2,1,0:T(8,128)(2,1)}, u32[]{:S(2)}) copy-start(bf16[1,768,2560]{2,1,0:T(8,128)(2,1)} %param.20) | copy-start | bytes 11796484
  90.5 10.3 %collective-permute-start.1 = (bf16[256,2560]{1,0:T(8,128)(2,1)S(1)}, bf16[256,2560]{1,0:T(8,128)(2,1)S(1)}, u32[]{:S(2)}, u32[]{:S(2)}) collective-permute-start(bf16[256,2560]{1,0:T(8,128)(2,1)S(1)} %slice.17), channel_id=1, source_target_pairs={{0,1},{1,0},{2,3},{3,2},{4,5},{5,4},{6,7},{7,6},{8,9},{9,8},{10,11... | collective-permute-start | bytes 3932168 | tf_op jit(solution)/shard_map/ppermute | solution.py:63
  100.7 3.1 %collective-permute-start.5 = (bf16[256,2560]{1,0:T(8,128)(2,1)S(1)}, bf16[256,2560]{1,0:T(8,128)(2,1)S(1)}, u32[]{:S(2)}, u32[]{:S(2)}) collective-permute-start(bf16[256,2560]{1,0:T(8,128)(2,1)S(1)} %slice.19), channel_id=1, source_target_pairs={{0,1},{1,0},{2,3},{3,2},{4,5},{5,4},{6,7},{7,6},{8,9},{9,8},{10,11... | collective-permute-start | bytes 3932168 | tf_op jit(solution)/shard_map/ppermute | solution.py:63
  126.7 3.9 %copy-start.5 = (s32[64,6]{0,1:T(8,128)S(1)}, s32[64,6]{0,1:T(8,128)}, u32[]{:S(2)}) copy-start(s32[64,6]{0,1:T(8,128)} %param.19) | copy-start | bytes 4612
  126.7 3.9 %copy-start.3 = (bf16[2560,16]{0,1:T(8,128)(2,1)S(1)}, bf16[2560,16]{0,1:T(8,128)(2,1)}, u32[]{:S(2)}) copy-start(bf16[2560,16]{0,1:T(8,128)(2,1)} %param.18) | copy-start | bytes 245764
  126.7 30.2 %all-to-all-start.3 = ((bf16[16,16,2560]{2,1,0:T(8,128)(2,1)}), bf16[16,16,2560]{2,1,0:T(8,128)(2,1)S(1)}, u32[]{:S(2)}, u32[]{:S(2)}) async-start(bf16[16,16,2560]{2,1,0:T(8,128)(2,1)} %bitcast.80), calls=%async_computation.3 | async-start | bytes 2621440 | tf_op jit(solution)/shard_map/all_to_all | solution.py:21
  134.2 1.8 %copy-start.6 = (bf16[2560]{0:T(1024)(128)(2,1)S(1)}, bf16[2560]{0:T(1024)(128)(2,1)}, u32[]{:S(2)}) copy-start(bf16[2560]{0:T(1024)(128)(2,1)} %param.23) | copy-start | bytes 15364
  135.3 22.8 %collective-permute-start.6 = (bf16[64,2560]{1,0:T(8,128)(2,1)}, bf16[64,2560]{1,0:T(8,128)(2,1)S(1)}, u32[]{:S(2)}, u32[]{:S(2)}) collective-permute-start(bf16[64,2560]{1,0:T(8,128)(2,1)} %fusion.10), channel_id=1, source_target_pairs={{0,16},{1,17},{2,18},{3,19},{4,20},{5,21},{6,22},{7,23},{8,24},{9,... | collective-permute-start | bytes 983048 | tf_op jit(solution)/shard_map/ppermute | solution.py:141

commit v3 on v2

--- a/solution.py
+++ b/solution.py
@@ -56,10 +56,13 @@
     ).astype(jnp.bfloat16)
 
 
-def run_expert(mine, swap, weights):
-    rows = mine.shape[0]
-    other = lax.ppermute(mine, "expert", swap)
-    parts = expert_half(jnp.concatenate([mine, other], axis=0), *weights).astype(jnp.bfloat16)
+def both_cores(mine, swap):
+    return jnp.concatenate([mine, lax.ppermute(mine, "expert", swap)], axis=0)
+
+
+def run_expert(inputs, swap, weights):
+    rows = inputs.shape[0] // 2
+    parts = expert_half(inputs, *weights).astype(jnp.bfloat16)
     arrived = lax.ppermute(parts[rows:], "expert", swap)
     return (parts[:rows].astype(jnp.float32) + arrived.astype(jnp.float32)).astype(jnp.bfloat16)
 
@@ -130,9 +133,11 @@
     blocks = (half, slot_total // half, feature_count)
     flat = (slot_total, feature_count)
     near_in = exchange(fill_slots(near_taken, normed).reshape(blocks), sides).reshape(flat)
-    far_in = exchange(fill_slots(far_taken, far_normed).reshape(blocks), sides).reshape(flat)
+    far_slots = fill_slots(far_taken, far_normed).reshape(blocks)
+    near_in, far_slots = lax.optimization_barrier((both_cores(near_in, swap), far_slots))
+    far_in = exchange(far_slots, sides).reshape(flat)
     near_sum = run_expert(near_in, swap, weights)
-    far_sum = run_expert(far_in, swap, weights)
+    far_sum = run_expert(both_cores(far_in, swap), swap, weights)
     near_sum, far_sum = lax.optimization_barrier((near_sum, far_sum))
     far_out = exchange(far_sum.reshape(blocks), sides).reshape(flat)
     near_out = exchange(near_sum.reshape(blocks), sides).reshape(flat)

time: 161 us -> 168 us (1.043)
  blocking collectives: 22.5 us -> 45 us
  waiting for transfers between devices: 71.2 us -> 61.1 us
  starting transfers between devices: 26.5 us -> 20.5 us
    all_to_all x1 -> x2, blocking collectives: 22.5 us -> 45 us  [exchange(): lax.all_to_all(blocks, 'expert', split_axis=0, concat_axis=0, axis_index_...]
    all_to_all x4 -> x3, waiting for transfers between devices: 41.4 us -> 35.4 us  [exchange(): lax.all_to_all(blocks, 'expert', split_axis=0, concat_axis=0, axis_index_...]
    all_to_all x4 -> x3, starting transfers between devices: 20.3 us -> 15.5 us  [exchange(): lax.all_to_all(blocks, 'expert', split_axis=0, concat_axis=0, axis_index_...]
    ppermute x1, waiting for transfers between devices: 20.8 us -> 16.6 us  [body(): far_normed = lax.ppermute(normed, 'expert', across)]
  transfers between devices with their start and end apart: 11 -> 10, of which waited for: 6 -> 5; matrix products, arithmetic and copies ran while one was open for 19% -> 20% of each run, Pallas kernels for 0% -> 0%
where the time goes in v3:
time: 168 us; the launch traced here: 167 us
  waiting for transfers between devices  61.1 us (36%)
  blocking collectives  45 us (27%)
  matrix products  32 us (19%)
  starting transfers between devices  20.5 us (12%)
  other arithmetic  5.15 us (3%)
  local copies, waits for them, and re-layouts  2.21 us (1%)
    all_to_all x2, blocking collectives, exchange(): lax.all_to_all(blocks, 'expert', split_axis=0, concat_axis=0, axis_index_...  45 us
    all_to_all x3, waiting for transfers between devices, exchange(): lax.all_to_all(blocks, 'expert', split_axis=0, concat_axis=0, axis_index_...  35.4 us
    ppermute x1, waiting for transfers between devices, body(): far_normed = lax.ppermute(normed, 'expert', across)  16.6 us
    all_to_all x3, starting transfers between devices, exchange(): lax.all_to_all(blocks, 'expert', split_axis=0, concat_axis=0, axis_index_...  15.5 us
    dot_general x2, matrix products, expert_half(): lax.dot_general(inputs, gate_rows, contract, preferred_element_type=jnp.f...  9.4 us
    dot_general x2, matrix products, expert_half(): lax.dot_general(inputs, up_rows, contract, preferred_element_type=jnp.flo...  8.67 us
    ppermute x1, waiting for transfers between devices, body(): far_routes = lax.ppermute(expert_routes, 'expert', across)  7.44 us
    dot_general x2, matrix products, expert_half(): return jnp.dot(active, down_rows, preferred_element_type=jnp.float32)  4.4 us
  transfers between devices with their start and end apart: 10, of which 5 were waited for; matrix products, arithmetic and copies ran while one was open for 20% of the time, Pallas kernels for 0%

profile of v3, /device:TPU:0, one launch (start us, length us, event | category | flops | bytes accessed | tf_op | source)
XLA Modules:
  0.0 166.9 jit_solution(14775528515085206473)
XLA Ops:
  2.9 7.3 %all-to-all-start = ((bf16[32,2,2560]{2,1,0:T(2,128)(2,1)}), bf16[32,2,2560]{2,1,0:T(2,128)(2,1)S(1)}, u32[]{:S(2)}, u32[]{:S(2)}) async-start(bf16[32,2,2560]{2,1,0:T(2,128)(2,1)} %broadcast_in_dim.45), calls=%async_computation | async-start | bytes 655360 | tf_op jit(solution)/shard_map/all_to_all | solution.py:21
  10.2 2.7 %collective-permute-start.1 = (s32[64,6]{0,1:T(8,128)}, s32[64,6]{0,1:T(8,128)S(1)}, u32[]{:S(2)}, u32[]{:S(2)}) collective-permute-start(s32[64,6]{0,1:T(8,128)} %param.19), channel_id=1, source_target_pairs={{0,16},{1,17},{2,18},{3,19},{4,20},{5,21},{6,22},{7,23},{8,24},{9,... | collective-permute-start | bytes 4616 | tf_op jit(solution)/shard_map/ppermute | solution.py:128
  13.8 7.4 %collective-permute-done.1 = s32[64,6]{0,1:T(8,128)S(1)} collective-permute-done((s32[64,6]{0,1:T(8,128)}, s32[64,6]{0,1:T(8,128)S(1)}, u32[]{:S(2)}, u32[]{:S(2)}) %collective-permute-start.1) | collective-permute-done | bytes 1568 | tf_op jit(solution)/shard_map/ppermute | solution.py:128
  23.7 22.5 %all_to_all.25 = bf16[16,16,2560]{2,1,0:T(8,128)(2,1)S(1)} all-to-all(bf16[16,16,2560]{2,1,0:T(8,128)(2,1)S(1)} %bitcast.84), channel_id=1, replica_groups={{0,1,2,3,4,5,6,7,8,9,10,11,12,13,14,15},{16,17,18,19,20,21,22,23,24,25,..., dimensions={0} | all-to-all | bytes 2621440 | tf_op jit(solution)/shard_map/all_to_all | solution.py:21
  46.3 1.4 collective-permute-start.2
  47.7 16.6 %collective-permute-done.2 = bf16[64,2560]{1,0:T(8,128)(2,1)S(1)} collective-permute-done((bf16[64,2560]{1,0:T(8,128)(2,1)S(1)}, bf16[64,2560]{1,0:T(8,128)(2,1)S(1)}, u32[]{:S(2)}, u32[]{:S(2)}) %collective-permute-start.2) | collective-permute-done | bytes 327712 | tf_op jit(solution)/shard_map/ppermute | solution.py:129
  64.3 1.5 convolution_convert_fusion.2
  66.0 4.4 %all-to-all-start.2 = ((bf16[16,16,2560]{2,1,0:T(8,128)(2,1)}), bf16[16,16,2560]{2,1,0:T(8,128)(2,1)}, u32[]{:S(2)}, u32[]{:S(2)}) async-start(bf16[16,16,2560]{2,1,0:T(8,128)(2,1)} %bitcast.12), calls=%async_computation.2 | async-start | bytes 2621440 | tf_op jit(solution)/shard_map/all_to_all | solution.py:21
  70.4 5.5 %fusion.8 = f32[512,768]{1,0:T(8,128)} fusion(bf16[512,2560]{1,0:T(8,128)(2,1)S(1)} %pad_maximum_fusion, bf16[1,768,2560]{2,1,0:T(8,128)(2,1)} %param.20), kind=kOutput, calls=%fused_computation.10 | convolution fusion | flops 2013265920 | bytes 8126464 | tf_op jit(solution)/shard_map/dot_general | solution.py:13
  75.9 13.8 %all-to-all-done.2 = bf16[16,16,2560]{2,1,0:T(8,128)(2,1)} async-done(((bf16[16,16,2560]{2,1,0:T(8,128)(2,1)}), bf16[16,16,2560]{2,1,0:T(8,128)(2,1)}, u32[]{:S(2)}, u32[]{:S(2)}) %all-to-all-start.2) | async-done | bytes 1310752 | tf_op jit(solution)/shard_map/all_to_all | solution.py:21
  89.8 5.0 %multiply_convert_fusion.1 = bf16[512,768]{1,0:T(8,128)(2,1)S(1)} fusion(f32[512,768]{1,0:T(8,128)} %fusion.8, bf16[512,2560]{1,0:T(8,128)(2,1)S(1)} %pad_maximum_fusion, bf16[1,768,2560]{2,1,0:T(8,128)(2,1)} %param.21), kind=kOutput, calls=%fused_computation.24 | convolution fusion | flops 2015625216 | bytes 8912896 | tf_op jit(solution)/shard_map/dot_general | solution.py:14
  94.8 2.2 %convolution_convert_fusion.1 = bf16[512,2560]{1,0:T(8,128)(2,1)S(1)} fusion(bf16[512,768]{1,0:T(8,128)(2,1)S(1)} %multiply_convert_fusion.1, bf16[1,768,2560]{2,1,0:T(8,128)(2,1)S(1)} %copy-done.11), kind=kOutput, calls=%fused_computation.1 | convolution fusion | flops 2014576640 | bytes 7340032 | tf_op jit(solution)/shard_map/dot_general | solution.py:17
  97.9 3.9 %fusion.6 = f32[512,768]{1,0:T(8,128)S(1)} fusion(bf16[1,768,2560]{2,1,0:T(8,128)(2,1)S(1)} %copy-done.9, bf16[256,2560]{1,0:T(8,128)(2,1)S(1)} %collective-permute-done.4, bf16[256,2560]{1,0:T(8,128)(2,1)} %bitcast.16), kind=kOutput, calls=%fused_computation.8 | convolution fusion | flops 2018508800 | bytes 8126464 | tf_op jit(solution)/shard_map/dot_general | solution.py:13
  101.8 3.6 %multiply_convert_fusion = bf16[512,768]{1,0:T(8,128)(2,1)S(1)} fusion(f32[512,768]{1,0:T(8,128)S(1)} %fusion.6, bf16[1,768,2560]{2,1,0:T(8,128)(2,1)S(1)} %copy-done.10, bf16[256,2560]{1,0:T(8,128)(2,1)S(1)} %collective-permute-done.4, bf16[256,2560]{1,0:T(8,128)(2,1)} %bitcast.16), kind=kOutput, calls=%fused_computation.23 | convolution fusion | flops 2020868096 | bytes 8912896 | tf_op jit(solution)/shard_map/dot_general | solution.py:14
  105.5 2.2 %convolution_convert_fusion = bf16[512,2560]{1,0:T(8,128)(2,1)S(1)} fusion(bf16[512,768]{1,0:T(8,128)(2,1)S(1)} %multiply_convert_fusion, bf16[1,768,2560]{2,1,0:T(8,128)(2,1)S(1)} %copy-done.11), kind=kOutput, calls=%fused_computation | convolution fusion | flops 2014576640 | bytes 7340032 | tf_op jit(solution)/shard_map/dot_general | solution.py:17
  107.8 1.4 add_convert_fusion.1
  109.2 1.6 collective-permute-done.5
  111.2 22.4 %all_to_all.26 = bf16[16,16,2560]{2,1,0:T(8,128)(2,1)S(1)} all-to-all(bf16[16,16,2560]{2,1,0:T(8,128)(2,1)S(1)} %bitcast.86), channel_id=1, replica_groups={{0,1,2,3,4,5,6,7,8,9,10,11,12,13,14,15},{16,17,18,19,20,21,22,23,24,25,..., dimensions={0} | all-to-all | bytes 2621440 | tf_op jit(solution)/shard_map/all_to_all | solution.py:21
  133.6 3.8 %all-to-all-start.3 = ((bf16[16,16,2560]{2,1,0:T(8,128)(2,1)}), bf16[16,16,2560]{2,1,0:T(8,128)(2,1)S(1)}, u32[]{:S(2)}, u32[]{:S(2)}) async-start(bf16[16,16,2560]{2,1,0:T(8,128)(2,1)} %bitcast.85), calls=%async_computation.3 | async-start | bytes 2621440 | tf_op jit(solution)/shard_map/all_to_all | solution.py:21
  137.5 1.2 fusion.49
  138.8 1.2 fusion.48
  142.2 21.6 %all-to-all-done.3 = bf16[16,16,2560]{2,1,0:T(8,128)(2,1)S(1)} async-done(((bf16[16,16,2560]{2,1,0:T(8,128)(2,1)}), bf16[16,16,2560]{2,1,0:T(8,128)(2,1)S(1)}, u32[]{:S(2)}, u32[]{:S(2)}) %all-to-all-start.3) | async-done | bytes 1310752 | tf_op jit(solution)/shard_map/all_to_all | solution.py:21
  163.8 1.2 fusion.51
  165.0 1.2 multiply_reduce_fusion
  (68 shorter events, 10.0 us)
Async XLA Ops:
  0.6 0.9 copy-start
  0.6 21.9 %copy-start.8 = (s32[4]{0:T(128)S(1)}, s32[4]{0:T(128)}, u32[]{:S(2)}) copy-start(s32[4]{0:T(128)} %param.15) | copy-start | bytes 52
  0.7 21.9 %copy-start.7 = (s32[1,64]{1,0:T(1,128)S(1)}, s32[1,64]{1,0:T(1,128)}, u32[]{:S(2)}) copy-start(s32[1,64]{1,0:T(1,128)} %param.16) | copy-start | bytes 772
  0.7 21.9 %copy-start.4 = (bf16[64,2560]{1,0:T(8,128)(2,1)S(1)}, bf16[64,2560]{1,0:T(8,128)(2,1)}, u32[]{:S(2)}) copy-start(bf16[64,2560]{1,0:T(8,128)(2,1)} %param.12) | copy-start | bytes 983044
  2.9 19.4 %all-to-all-start = ((bf16[32,2,2560]{2,1,0:T(2,128)(2,1)}), bf16[32,2,2560]{2,1,0:T(2,128)(2,1)S(1)}, u32[]{:S(2)}, u32[]{:S(2)}) async-start(bf16[32,2,2560]{2,1,0:T(2,128)(2,1)} %broadcast_in_dim.45), calls=%async_computation | async-start | bytes 655360 | tf_op jit(solution)/shard_map/all_to_all | solution.py:21
  10.2 11.0 %collective-permute-start.1 = (s32[64,6]{0,1:T(8,128)}, s32[64,6]{0,1:T(8,128)S(1)}, u32[]{:S(2)}, u32[]{:S(2)}) collective-permute-start(s32[64,6]{0,1:T(8,128)} %param.19), channel_id=1, source_target_pairs={{0,16},{1,17},{2,18},{3,19},{4,20},{5,21},{6,22},{7,23},{8,24},{9,... | collective-permute-start | bytes 4616 | tf_op jit(solution)/shard_map/ppermute | solution.py:128
  23.2 23.0 %copy-start.1 = (bf16[64,2560]{1,0:T(8,128)(2,1)}, bf16[64,2560]{1,0:T(8,128)(2,1)S(1)}, u32[]{:S(2)}) copy-start(bf16[64,2560]{1,0:T(8,128)(2,1)S(1)} %multiply_convert_fusion.2) | copy-start | bytes 983044
  46.3 19.6 %collective-permute-start = (bf16[256,2560]{1,0:T(8,128)(2,1)S(1)}, bf16[256,2560]{1,0:T(8,128)(2,1)S(1)}, u32[]{:S(2)}, u32[]{:S(2)}) collective-permute-start(bf16[256,2560]{1,0:T(8,128)(2,1)S(1)} %bitcast.82), channel_id=1, source_target_pairs={{0,1},{1,0},{2,3},{3,2},{4,5},{5,4},{6,7},{7,6},{8,9},{9,8},{10,11... | collective-permute-start | bytes 3932168 | tf_op jit(solution)/shard_map/ppermute | solution.py:60
  46.3 18.0 %collective-permute-start.2 = (bf16[64,2560]{1,0:T(8,128)(2,1)S(1)}, bf16[64,2560]{1,0:T(8,128)(2,1)S(1)}, u32[]{:S(2)}, u32[]{:S(2)}) collective-permute-start(bf16[64,2560]{1,0:T(8,128)(2,1)S(1)} %multiply_convert_fusion.2), channel_id=1, source_target_pairs={{0,16},{1,17},{2,18},{3,19},{4,20},{5,21},{6,22},{7,23},{8,24},{9,... | collective-permute-start | bytes 983048 | tf_op jit(solution)/shard_map/ppermute | solution.py:129
  64.3 1.5 copy-start.2
  66.0 23.8 %all-to-all-start.2 = ((bf16[16,16,2560]{2,1,0:T(8,128)(2,1)}), bf16[16,16,2560]{2,1,0:T(8,128)(2,1)}, u32[]{:S(2)}, u32[]{:S(2)}) async-start(bf16[16,16,2560]{2,1,0:T(8,128)(2,1)} %bitcast.12), calls=%async_computation.2 | async-start | bytes 2621440 | tf_op jit(solution)/shard_map/all_to_all | solution.py:21
  89.8 5.1 %copy-start.11 = (bf16[1,768,2560]{2,1,0:T(8,128)(2,1)S(1)}, bf16[1,768,2560]{2,1,0:T(8,128)(2,1)}, u32[]{:S(2)}) copy-start(bf16[1,768,2560]{2,1,0:T(8,128)(2,1)} %param.22) | copy-start | bytes 11796484
  89.8 8.1 %collective-permute-start.4 = (bf16[256,2560]{1,0:T(8,128)(2,1)}, bf16[256,2560]{1,0:T(8,128)(2,1)S(1)}, u32[]{:S(2)}, u32[]{:S(2)}) collective-permute-start(bf16[256,2560]{1,0:T(8,128)(2,1)} %bitcast.16), channel_id=1, source_target_pairs={{0,1},{1,0},{2,3},{3,2},{4,5},{5,4},{6,7},{7,6},{8,9},{9,8},{10,11... | collective-permute-start | bytes 3932168 | tf_op jit(solution)/shard_map/ppermute | solution.py:60
  94.8 3.1 %copy-start.9 = (bf16[1,768,2560]{2,1,0:T(8,128)(2,1)S(1)}, bf16[1,768,2560]{2,1,0:T(8,128)(2,1)}, u32[]{:S(2)}) copy-start(bf16[1,768,2560]{2,1,0:T(8,128)(2,1)} %param.20) | copy-start | bytes 11796484
  97.1 4.7 %copy-start.10 = (bf16[1,768,2560]{2,1,0:T(8,128)(2,1)S(1)}, bf16[1,768,2560]{2,1,0:T(8,128)(2,1)}, u32[]{:S(2)}) copy-start(bf16[1,768,2560]{2,1,0:T(8,128)(2,1)} %param.21) | copy-start | bytes 11796484
  97.2 10.7 %collective-permute-start.3 = (bf16[256,2560]{1,0:T(8,128)(2,1)S(1)}, bf16[256,2560]{1,0:T(8,128)(2,1)S(1)}, u32[]{:S(2)}, u32[]{:S(2)}) collective-permute-start(bf16[256,2560]{1,0:T(8,128)(2,1)S(1)} %slice.17), channel_id=1, source_target_pairs={{0,1},{1,0},{2,3},{3,2},{4,5},{5,4},{6,7},{7,6},{8,9},{9,8},{10,11... | collective-permute-start | bytes 3932168 | tf_op jit(solution)/shard_map/ppermute | solution.py:66
  107.8 3.1 %collective-permute-start.5 = (bf16[256,2560]{1,0:T(8,128)(2,1)S(1)}, bf16[256,2560]{1,0:T(8,128)(2,1)S(1)}, u32[]{:S(2)}, u32[]{:S(2)}) collective-permute-start(bf16[256,2560]{1,0:T(8,128)(2,1)S(1)} %slice.19), channel_id=1, source_target_pairs={{0,1},{1,0},{2,3},{3,2},{4,5},{5,4},{6,7},{7,6},{8,9},{9,8},{10,11... | collective-permute-start | bytes 3932168 | tf_op jit(solution)/shard_map/ppermute | solution.py:66
  133.6 3.9 %copy-start.5 = (s32[64,6]{0,1:T(8,128)S(1)}, s32[64,6]{0,1:T(8,128)}, u32[]{:S(2)}) copy-start(s32[64,6]{0,1:T(8,128)} %param.19) | copy-start | bytes 4612
  133.6 3.9 %copy-start.3 = (bf16[2560,16]{0,1:T(8,128)(2,1)S(1)}, bf16[2560,16]{0,1:T(8,128)(2,1)}, u32[]{:S(2)}) copy-start(bf16[2560,16]{0,1:T(8,128)(2,1)} %param.18) | copy-start | bytes 245764
  133.6 30.2 %all-to-all-start.3 = ((bf16[16,16,2560]{2,1,0:T(8,128)(2,1)}), bf16[16,16,2560]{2,1,0:T(8,128)(2,1)S(1)}, u32[]{:S(2)}, u32[]{:S(2)}) async-start(bf16[16,16,2560]{2,1,0:T(8,128)(2,1)} %bitcast.85), calls=%async_computation.3 | async-start | bytes 2621440 | tf_op jit(solution)/shard_map/all_to_all | solution.py:21
  141.1 1.1 copy-start.6
  142.2 22.8 %collective-permute-start.6 = (bf16[64,2560]{1,0:T(8,128)(2,1)}, bf16[64,2560]{1,0:T(8,128)(2,1)S(1)}, u32[]{:S(2)}, u32[]{:S(2)}) collective-permute-start(bf16[64,2560]{1,0:T(8,128)(2,1)} %fusion.10), channel_id=1, source_target_pairs={{0,16},{1,17},{2,18},{3,19},{4,20},{5,21},{6,22},{7,23},{8,24},{9,... | collective-permute-start | bytes 983048 | tf_op jit(solution)/shard_map/ppermute | solution.py:146

commit v4 on v3

--- a/solution.py
+++ b/solution.py
@@ -14,7 +14,7 @@
     up_value = lax.dot_general(inputs, up_rows, contract, preferred_element_type=jnp.float32)
     active = (jax.nn.silu(gate_value) * up_value).astype(jnp.bfloat16)
     active = lax.optimization_barrier(active)
-    return jnp.dot(active, down_rows, preferred_element_type=jnp.float32)
+    return jnp.dot(active, down_rows, preferred_element_type=jnp.float32).astype(jnp.bfloat16)
 
 
 def exchange(blocks, groups=None):
@@ -60,9 +60,8 @@
     return jnp.concatenate([mine, lax.ppermute(mine, "expert", swap)], axis=0)
 
 
-def run_expert(inputs, swap, weights):
-    rows = inputs.shape[0] // 2
-    parts = expert_half(inputs, *weights).astype(jnp.bfloat16)
+def sum_cores(parts, swap):
+    rows = parts.shape[0] // 2
     arrived = lax.ppermute(parts[rows:], "expert", swap)
     return (parts[:rows].astype(jnp.float32) + arrived.astype(jnp.float32)).astype(jnp.bfloat16)
 
@@ -134,10 +133,13 @@
     flat = (slot_total, feature_count)
     near_in = exchange(fill_slots(near_taken, normed).reshape(blocks), sides).reshape(flat)
     far_slots = fill_slots(far_taken, far_normed).reshape(blocks)
+    near_in, far_slots = lax.optimization_barrier((near_in, far_slots))
     near_in, far_slots = lax.optimization_barrier((both_cores(near_in, swap), far_slots))
     far_in = exchange(far_slots, sides).reshape(flat)
-    near_sum = run_expert(near_in, swap, weights)
-    far_sum = run_expert(both_cores(far_in, swap), swap, weights)
+    near_parts = expert_half(near_in, *weights)
+    near_parts, far_in = lax.optimization_barrier((near_parts, far_in))
+    near_sum = sum_cores(near_parts, swap)
+    far_sum = sum_cores(expert_half(both_cores(far_in, swap), *weights), swap)
     near_sum, far_sum = lax.optimization_barrier((near_sum, far_sum))
     far_out = exchange(far_sum.reshape(blocks), sides).reshape(flat)
     near_out = exchange(near_sum.reshape(blocks), sides).reshape(flat)

time: 168 us -> 155 us (0.923)
  blocking collectives: 45 us -> 22.7 us
  waiting for transfers between devices: 61.1 us -> 65.4 us
  local copies, waits for them, and re-layouts: 2.21 us -> 5.71 us
  matrix products: 32 us -> 29.7 us
  starting transfers between devices: 20.5 us -> 22.8 us
    all_to_all x2 -> x1, blocking collectives: 45 us -> 22.7 us  [exchange(): lax.all_to_all(blocks, 'expert', split_axis=0, concat_axis=0, axis_index_...]
    ppermute x1, waiting for transfers between devices: 7.44 us -> 0.01 us  [body(): far_routes = lax.ppermute(expert_routes, 'expert', across)]
    ppermute x1, waiting for transfers between devices: 16.6 us -> 21.8 us  [body(): far_normed = lax.ppermute(normed, 'expert', across)]
    all_to_all x3 -> x4, waiting for transfers between devices: 35.4 us -> 39.5 us  [exchange(): lax.all_to_all(blocks, 'expert', split_axis=0, concat_axis=0, axis_index_...]
    dot_general x2, matrix products: 8.67 us -> 4.61 us  [expert_half(): lax.dot_general(inputs, up_rows, contract, preferred_element_type=jnp.flo...]
    ppermute x2, waiting for transfers between devices: 0.01 us -> 3.99 us  [both_cores(): return jnp.concatenate([mine, lax.ppermute(mine, 'expert', swap)], axis=0)]
    unnamed x25 -> x30, local copies, waits for them, and re-layouts: 0.93 us -> 3.03 us
    dot_general x2, matrix products: 9.4 us -> 7.5 us  [expert_half(): lax.dot_general(inputs, gate_rows, contract, preferred_element_type=jnp.f...]
  transfers between devices with their start and end apart: 10 -> 11, of which waited for: 5 -> 8; matrix products, arithmetic and copies ran while one was open for 20% -> 21% of each run, Pallas kernels for 0% -> 0%
where the time goes in v4:
time: 155 us; the launch traced here: 154 us
  waiting for transfers between devices  65.4 us (42%)
  matrix products  29.7 us (19%)
  starting transfers between devices  22.8 us (15%)
  blocking collectives  22.7 us (15%)
  other arithmetic  6.73 us (4%)
  local copies, waits for them, and re-layouts  5.71 us (4%)
    all_to_all x4, waiting for transfers between devices, exchange(): lax.all_to_all(blocks, 'expert', split_axis=0, concat_axis=0, axis_index_...  39.5 us
    all_to_all x1, blocking collectives, exchange(): lax.all_to_all(blocks, 'expert', split_axis=0, concat_axis=0, axis_index_...  22.7 us
    ppermute x1, waiting for transfers between devices, body(): far_normed = lax.ppermute(normed, 'expert', across)  21.8 us
    all_to_all x4, starting transfers between devices, exchange(): lax.all_to_all(blocks, 'expert', split_axis=0, concat_axis=0, axis_index_...  15.6 us
    dot_general x2, matrix products, expert_half(): lax.dot_general(inputs, gate_rows, contract, preferred_element_type=jnp.f...  7.5 us
    dot_general x2, matrix products, expert_half(): jnp.dot(active, down_rows, preferred_element_type=jnp.float32)  5.91 us
    dot_general x2, matrix products, expert_half(): lax.dot_general(inputs, up_rows, contract, preferred_element_type=jnp.flo...  4.61 us
    ppermute x1, starting transfers between devices, body(): far_routes = lax.ppermute(expert_routes, 'expert', across)  4.1 us
  transfers between devices with their start and end apart: 11, of which 8 were waited for; matrix products, arithmetic and copies ran while one was open for 21% of the time, Pallas kernels for 0%

profile of v4, /device:TPU:0, one launch (start us, length us, event | category | flops | bytes accessed | tf_op | source)
XLA Modules:
  0.0 154.0 jit_solution(270031811034518296)
XLA Ops:
  0.6 4.1 %collective-permute-start = (s32[64,6]{0,1:T(8,128)}, s32[64,6]{0,1:T(8,128)S(1)}, u32[]{:S(2)}, u32[]{:S(2)}) collective-permute-start(s32[64,6]{0,1:T(8,128)} %param.19), channel_id=1, source_target_pairs={{0,16},{1,17},{2,18},{3,19},{4,20},{5,21},{6,22},{7,23},{8,24},{9,... | collective-permute-start | bytes 4616 | tf_op jit(solution)/shard_map/ppermute | solution.py:127
  6.8 3.8 %all-to-all-start = ((bf16[32,2,2560]{2,1,0:T(2,128)(2,1)}), bf16[32,2,2560]{2,1,0:T(2,128)(2,1)S(1)}, u32[]{:S(2)}, u32[]{:S(2)}) async-start(bf16[32,2,2560]{2,1,0:T(2,128)(2,1)} %broadcast_in_dim.45), calls=%async_computation | async-start | bytes 655360 | tf_op jit(solution)/shard_map/all_to_all | solution.py:21
  12.7 10.0 %all-to-all-done = bf16[32,2,2560]{2,1,0:T(2,128)(2,1)S(1)} async-done(((bf16[32,2,2560]{2,1,0:T(2,128)(2,1)}), bf16[32,2,2560]{2,1,0:T(2,128)(2,1)S(1)}, u32[]{:S(2)}, u32[]{:S(2)}) %all-to-all-start) | async-done | bytes 327712 | tf_op jit(solution)/shard_map/all_to_all | solution.py:21
  22.8 1.5 multiply_reduce_fusion.1
  24.5 1.6 %convolution_convert_fusion.3 = bf16[256,2560]{1,0:T(8,128)(2,1)} fusion(pred[64,256]{0,1:T(32,128)(4,1)S(1)} %get-tuple-element.33, bf16[64,2560]{1,0:T(8,128)(2,1)S(1)} %multiply_convert_fusion.2), kind=kOutput, calls=%fused_computation.13 | convolution fusion | flops 84541440 | bytes 1654784 | tf_op jit(solution)/shard_map/dot_general | solution.py:54
  26.1 3.7 %all-to-all-start.1 = ((bf16[16,16,2560]{2,1,0:T(8,128)(2,1)}), bf16[16,16,2560]{2,1,0:T(8,128)(2,1)S(1)}, u32[]{:S(2)}, u32[]{:S(2)}) async-start(bf16[16,16,2560]{2,1,0:T(8,128)(2,1)} %bitcast.8), calls=%async_computation.1 | async-start | bytes 2621440 | tf_op jit(solution)/shard_map/all_to_all | solution.py:21
  30.1 21.8 %collective-permute-done.1 = bf16[64,2560]{1,0:T(8,128)(2,1)S(1)} collective-permute-done((bf16[64,2560]{1,0:T(8,128)(2,1)S(1)}, bf16[64,2560]{1,0:T(8,128)(2,1)S(1)}, u32[]{:S(2)}, u32[]{:S(2)}) %collective-permute-start.1) | collective-permute-done | bytes 327712 | tf_op jit(solution)/shard_map/ppermute | solution.py:128
  52.6 1.5 %convolution_convert_fusion.2 = bf16[256,2560]{1,0:T(8,128)(2,1)} fusion(pred[64,256]{0,1:T(32,128)(4,1)S(1)} %get-tuple-element.32, bf16[64,2560]{1,0:T(8,128)(2,1)S(1)} %collective-permute-done.1), kind=kOutput, calls=%fused_computation.12 | convolution fusion | flops 84541440 | bytes 1654784 | tf_op jit(solution)/shard_map/dot_general | solution.py:54
  54.2 1.6 %all-to-all-done.1 = bf16[16,16,2560]{2,1,0:T(8,128)(2,1)S(1)} async-done(((bf16[16,16,2560]{2,1,0:T(8,128)(2,1)}), bf16[16,16,2560]{2,1,0:T(8,128)(2,1)S(1)}, u32[]{:S(2)}, u32[]{:S(2)}) %all-to-all-start.1) | async-done | bytes 1310752 | tf_op jit(solution)/shard_map/all_to_all | solution.py:21
  55.7 3.0 %collective-permute-done.2 = bf16[256,2560]{1,0:T(8,128)(2,1)S(1)} collective-permute-done((bf16[256,2560]{1,0:T(8,128)(2,1)S(1)}, bf16[256,2560]{1,0:T(8,128)(2,1)S(1)}, u32[]{:S(2)}, u32[]{:S(2)}) %collective-permute-start.2) | collective-permute-done | bytes 1310752 | tf_op jit(solution)/shard_map/ppermute | solution.py:60
  58.8 1.7 %pad_maximum_fusion = bf16[512,2560]{1,0:T(8,128)(2,1)} fusion(bf16[256,2560]{1,0:T(8,128)(2,1)S(1)} %collective-permute-done.2, bf16[256,2560]{1,0:T(8,128)(2,1)S(1)} %bitcast.85), kind=kLoop, calls=%fused_computation.19 | loop fusion | flops 5242880 | bytes 5242880 | tf_op jit(solution)/shard_map/concatenate | solution.py:60
  60.4 4.4 %all-to-all-start.2 = ((bf16[16,16,2560]{2,1,0:T(8,128)(2,1)}), bf16[16,16,2560]{2,1,0:T(8,128)(2,1)S(1)}, u32[]{:S(2)}, u32[]{:S(2)}) async-start(bf16[16,16,2560]{2,1,0:T(8,128)(2,1)} %bitcast.12), calls=%async_computation.2 | async-start | bytes 2621440 | tf_op jit(solution)/shard_map/all_to_all | solution.py:21
  64.8 5.3 %fusion.8 = f32[512,768]{1,0:T(8,128)S(1)} fusion(bf16[512,2560]{1,0:T(8,128)(2,1)} %pad_maximum_fusion, bf16[1,768,2560]{2,1,0:T(8,128)(2,1)} %param.20), kind=kOutput, calls=%fused_computation.10 | convolution fusion | flops 2013265920 | bytes 8126464 | tf_op jit(solution)/shard_map/dot_general | solution.py:13
  70.1 2.3 %multiply_convert_fusion.1 = bf16[512,768]{1,0:T(8,128)(2,1)S(1)} fusion(f32[512,768]{1,0:T(8,128)S(1)} %fusion.8, bf16[512,2560]{1,0:T(8,128)(2,1)S(1)} %copy-done.2, bf16[1,768,2560]{2,1,0:T(8,128)(2,1)S(1)} %copy-done.10), kind=kOutput, calls=%fused_computation.23 | convolution fusion | flops 2015625216 | bytes 8912896 | tf_op jit(solution)/shard_map/dot_general | solution.py:14
  72.5 3.7 %convolution_convert_fusion.1 = bf16[512,2560]{1,0:T(8,128)(2,1)} fusion(bf16[512,768]{1,0:T(8,128)(2,1)S(1)} %multiply_convert_fusion.1, bf16[1,768,2560]{2,1,0:T(8,128)(2,1)S(1)} %copy-done.12), kind=kOutput, calls=%fused_computation.1 | convolution fusion | flops 2014576640 | bytes 7340032 | tf_op jit(solution)/shard_map/dot_general | solution.py:17
  76.2 8.0 %all-to-all-done.2 = bf16[16,16,2560]{2,1,0:T(8,128)(2,1)S(1)} async-done(((bf16[16,16,2560]{2,1,0:T(8,128)(2,1)}), bf16[16,16,2560]{2,1,0:T(8,128)(2,1)S(1)}, u32[]{:S(2)}, u32[]{:S(2)}) %all-to-all-start.2) | async-done | bytes 1310752 | tf_op jit(solution)/shard_map/all_to_all | solution.py:21
  87.7 2.2 %fusion.6 = f32[512,768]{1,0:T(8,128)S(1)} fusion(bf16[512,2560]{1,0:T(8,128)(2,1)S(1)} %constant_dynamic-update-slice_fusion, bf16[1,768,2560]{2,1,0:T(8,128)(2,1)S(1)} %copy-done.9), kind=kOutput, calls=%fused_computation.8 | convolution fusion | flops 2013265920 | bytes 8126464 | tf_op jit(solution)/shard_map/dot_general | solution.py:13
  89.9 2.3 %multiply_convert_fusion = bf16[512,768]{1,0:T(8,128)(2,1)S(1)} fusion(f32[512,768]{1,0:T(8,128)S(1)} %fusion.6, bf16[512,2560]{1,0:T(8,128)(2,1)S(1)} %constant_dynamic-update-slice_fusion, bf16[1,768,2560]{2,1,0:T(8,128)(2,1)S(1)} %copy-done.11), kind=kOutput, calls=%fused_computation.22 | convolution fusion | flops 2015625216 | bytes 8912896 | tf_op jit(solution)/shard_map/dot_general | solution.py:14
  92.2 2.2 %convolution_convert_fusion = bf16[512,2560]{1,0:T(8,128)(2,1)S(1)} fusion(bf16[512,768]{1,0:T(8,128)(2,1)S(1)} %multiply_convert_fusion, bf16[1,768,2560]{2,1,0:T(8,128)(2,1)S(1)} %copy-done.13), kind=kOutput, calls=%fused_computation | convolution fusion | flops 2014576640 | bytes 7340032 | tf_op jit(solution)/shard_map/dot_general | solution.py:17
  96.2 1.5 add_convert_fusion.1
  98.1 22.7 %all_to_all.25 = bf16[16,16,2560]{2,1,0:T(8,128)(2,1)S(1)} all-to-all(bf16[16,16,2560]{2,1,0:T(8,128)(2,1)S(1)} %bitcast.89), channel_id=1, replica_groups={{0,1,2,3,4,5,6,7,8,9,10,11,12,13,14,15},{16,17,18,19,20,21,22,23,24,25,..., dimensions={0} | all-to-all | bytes 2621440 | tf_op jit(solution)/shard_map/all_to_all | solution.py:21
  120.8 3.7 %all-to-all-start.3 = ((bf16[16,16,2560]{2,1,0:T(8,128)(2,1)}), bf16[16,16,2560]{2,1,0:T(8,128)(2,1)S(1)}, u32[]{:S(2)}, u32[]{:S(2)}) async-start(bf16[16,16,2560]{2,1,0:T(8,128)(2,1)} %bitcast.88), calls=%async_computation.3 | async-start | bytes 2621440 | tf_op jit(solution)/shard_map/all_to_all | solution.py:21
  129.3 1.6 %collective-permute-start.6 = (bf16[64,2560]{1,0:T(8,128)(2,1)}, bf16[64,2560]{1,0:T(8,128)(2,1)S(1)}, u32[]{:S(2)}, u32[]{:S(2)}) collective-permute-start(bf16[64,2560]{1,0:T(8,128)(2,1)} %fusion.10), channel_id=1, source_target_pairs={{0,16},{1,17},{2,18},{3,19},{4,20},{5,21},{6,22},{7,23},{8,24},{9,... | collective-permute-start | bytes 983048 | tf_op jit(solution)/shard_map/ppermute | solution.py:148
  130.9 20.0 %all-to-all-done.3 = bf16[16,16,2560]{2,1,0:T(8,128)(2,1)S(1)} async-done(((bf16[16,16,2560]{2,1,0:T(8,128)(2,1)}), bf16[16,16,2560]{2,1,0:T(8,128)(2,1)S(1)}, u32[]{:S(2)}, u32[]{:S(2)}) %all-to-all-start.3) | async-done | bytes 1310752 | tf_op jit(solution)/shard_map/all_to_all | solution.py:21
  (75 shorter events, 18.9 us)
Async XLA Ops:
  0.6 4.8 %copy-start = (bf16[2,16,2560]{2,1,0:T(8,128)(2,1)S(1)}, bf16[2,16,2560]{2,1,0:T(8,128)(2,1)}, u32[]{:S(2)}) copy-start(bf16[2,16,2560]{2,1,0:T(8,128)(2,1)} %param.13) | copy-start | bytes 491524
  0.6 10.9 %collective-permute-start = (s32[64,6]{0,1:T(8,128)}, s32[64,6]{0,1:T(8,128)S(1)}, u32[]{:S(2)}, u32[]{:S(2)}) collective-permute-start(s32[64,6]{0,1:T(8,128)} %param.19), channel_id=1, source_target_pairs={{0,16},{1,17},{2,18},{3,19},{4,20},{5,21},{6,22},{7,23},{8,24},{9,... | collective-permute-start | bytes 4616 | tf_op jit(solution)/shard_map/ppermute | solution.py:127
  6.8 15.8 %all-to-all-start = ((bf16[32,2,2560]{2,1,0:T(2,128)(2,1)}), bf16[32,2,2560]{2,1,0:T(2,128)(2,1)S(1)}, u32[]{:S(2)}, u32[]{:S(2)}) async-start(bf16[32,2,2560]{2,1,0:T(2,128)(2,1)} %broadcast_in_dim.45), calls=%async_computation | async-start | bytes 655360 | tf_op jit(solution)/shard_map/all_to_all | solution.py:21
  24.5 29.7 %copy-start.1 = (bf16[64,2560]{1,0:T(8,128)(2,1)}, bf16[64,2560]{1,0:T(8,128)(2,1)S(1)}, u32[]{:S(2)}) copy-start(bf16[64,2560]{1,0:T(8,128)(2,1)S(1)} %multiply_convert_fusion.2) | copy-start | bytes 983044
  26.1 29.7 %all-to-all-start.1 = ((bf16[16,16,2560]{2,1,0:T(8,128)(2,1)}), bf16[16,16,2560]{2,1,0:T(8,128)(2,1)S(1)}, u32[]{:S(2)}, u32[]{:S(2)}) async-start(bf16[16,16,2560]{2,1,0:T(8,128)(2,1)} %bitcast.8), calls=%async_computation.1 | async-start | bytes 2621440 | tf_op jit(solution)/shard_map/all_to_all | solution.py:21
  29.8 22.1 %collective-permute-start.1 = (bf16[64,2560]{1,0:T(8,128)(2,1)S(1)}, bf16[64,2560]{1,0:T(8,128)(2,1)S(1)}, u32[]{:S(2)}, u32[]{:S(2)}) collective-permute-start(bf16[64,2560]{1,0:T(8,128)(2,1)S(1)} %multiply_convert_fusion.2), channel_id=1, source_target_pairs={{0,16},{1,17},{2,18},{3,19},{4,20},{5,21},{6,22},{7,23},{8,24},{9,... | collective-permute-start | bytes 983048 | tf_op jit(solution)/shard_map/ppermute | solution.py:128
  55.7 3.0 %collective-permute-start.2 = (bf16[256,2560]{1,0:T(8,128)(2,1)S(1)}, bf16[256,2560]{1,0:T(8,128)(2,1)S(1)}, u32[]{:S(2)}, u32[]{:S(2)}) collective-permute-start(bf16[256,2560]{1,0:T(8,128)(2,1)S(1)} %bitcast.84), channel_id=1, source_target_pairs={{0,1},{1,0},{2,3},{3,2},{4,5},{5,4},{6,7},{7,6},{8,9},{9,8},{10,11... | collective-permute-start | bytes 3932168 | tf_op jit(solution)/shard_map/ppermute | solution.py:60
  60.4 23.7 %all-to-all-start.2 = ((bf16[16,16,2560]{2,1,0:T(8,128)(2,1)}), bf16[16,16,2560]{2,1,0:T(8,128)(2,1)S(1)}, u32[]{:S(2)}, u32[]{:S(2)}) async-start(bf16[16,16,2560]{2,1,0:T(8,128)(2,1)} %bitcast.12), calls=%async_computation.2 | async-start | bytes 2621440 | tf_op jit(solution)/shard_map/all_to_all | solution.py:21
  64.8 5.3 %copy-start.2 = (bf16[512,2560]{1,0:T(8,128)(2,1)S(1)}, bf16[512,2560]{1,0:T(8,128)(2,1)}, u32[]{:S(2)}) copy-start(bf16[512,2560]{1,0:T(8,128)(2,1)} %pad_maximum_fusion) | copy-start | bytes 7864324
  64.8 5.3 %copy-start.10 = (bf16[1,768,2560]{2,1,0:T(8,128)(2,1)S(1)}, bf16[1,768,2560]{2,1,0:T(8,128)(2,1)}, u32[]{:S(2)}) copy-start(bf16[1,768,2560]{2,1,0:T(8,128)(2,1)} %param.21) | copy-start | bytes 11796484
  70.1 2.3 %copy-start.12 = (bf16[1,768,2560]{2,1,0:T(8,128)(2,1)S(1)}, bf16[1,768,2560]{2,1,0:T(8,128)(2,1)}, u32[]{:S(2)}) copy-start(bf16[1,768,2560]{2,1,0:T(8,128)(2,1)} %param.22) | copy-start | bytes 11796484
  84.1 3.0 %collective-permute-start.4 = (bf16[256,2560]{1,0:T(8,128)(2,1)S(1)}, bf16[256,2560]{1,0:T(8,128)(2,1)S(1)}, u32[]{:S(2)}, u32[]{:S(2)}) collective-permute-start(bf16[256,2560]{1,0:T(8,128)(2,1)S(1)} %bitcast.86), channel_id=1, source_target_pairs={{0,1},{1,0},{2,3},{3,2},{4,5},{5,4},{6,7},{7,6},{8,9},{9,8},{10,11... | collective-permute-start | bytes 3932168 | tf_op jit(solution)/shard_map/ppermute | solution.py:60
  85.5 2.1 %copy-start.9 = (bf16[1,768,2560]{2,1,0:T(8,128)(2,1)S(1)}, bf16[1,768,2560]{2,1,0:T(8,128)(2,1)}, u32[]{:S(2)}) copy-start(bf16[1,768,2560]{2,1,0:T(8,128)(2,1)} %param.20) | copy-start | bytes 11796484
  85.6 9.6 %collective-permute-start.3 = (bf16[256,2560]{1,0:T(8,128)(2,1)S(1)}, bf16[256,2560]{1,0:T(8,128)(2,1)S(1)}, u32[]{:S(2)}, u32[]{:S(2)}) collective-permute-start(bf16[256,2560]{1,0:T(8,128)(2,1)S(1)} %slice.13), channel_id=1, source_target_pairs={{0,1},{1,0},{2,3},{3,2},{4,5},{5,4},{6,7},{7,6},{8,9},{9,8},{10,11... | collective-permute-start | bytes 3932168 | tf_op jit(solution)/shard_map/ppermute | solution.py:65
  87.7 2.2 %copy-start.11 = (bf16[1,768,2560]{2,1,0:T(8,128)(2,1)S(1)}, bf16[1,768,2560]{2,1,0:T(8,128)(2,1)}, u32[]{:S(2)}) copy-start(bf16[1,768,2560]{2,1,0:T(8,128)(2,1)} %param.21) | copy-start | bytes 11796484
  89.9 2.3 %copy-start.13 = (bf16[1,768,2560]{2,1,0:T(8,128)(2,1)S(1)}, bf16[1,768,2560]{2,1,0:T(8,128)(2,1)}, u32[]{:S(2)}) copy-start(bf16[1,768,2560]{2,1,0:T(8,128)(2,1)} %param.22) | copy-start | bytes 11796484
  94.4 1.7 %copy-start.3 = (bf16[512,2560]{1,0:T(8,128)(2,1)S(1)}, bf16[512,2560]{1,0:T(8,128)(2,1)}, u32[]{:S(2)}) copy-start(bf16[512,2560]{1,0:T(8,128)(2,1)} %convolution_convert_fusion.1) | copy-start | bytes 7864324
  94.5 3.2 %collective-permute-start.5 = (bf16[256,2560]{1,0:T(8,128)(2,1)S(1)}, bf16[256,2560]{1,0:T(8,128)(2,1)S(1)}, u32[]{:S(2)}, u32[]{:S(2)}) collective-permute-start(bf16[256,2560]{1,0:T(8,128)(2,1)S(1)} %slice.17), channel_id=1, source_target_pairs={{0,1},{1,0},{2,3},{3,2},{4,5},{5,4},{6,7},{7,6},{8,9},{9,8},{10,11... | collective-permute-start | bytes 3932168 | tf_op jit(solution)/shard_map/ppermute | solution.py:65
  98.1 26.4 %copy-start.6 = (s32[64,6]{0,1:T(8,128)S(1)}, s32[64,6]{0,1:T(8,128)}, u32[]{:S(2)}) copy-start(s32[64,6]{0,1:T(8,128)} %param.19) | copy-start | bytes 4612
  98.1 26.5 %copy-start.5 = (bf16[2560,16]{0,1:T(8,128)(2,1)S(1)}, bf16[2560,16]{0,1:T(8,128)(2,1)}, u32[]{:S(2)}) copy-start(bf16[2560,16]{0,1:T(8,128)(2,1)} %param.18) | copy-start | bytes 245764
  120.8 30.0 %all-to-all-start.3 = ((bf16[16,16,2560]{2,1,0:T(8,128)(2,1)}), bf16[16,16,2560]{2,1,0:T(8,128)(2,1)S(1)}, u32[]{:S(2)}, u32[]{:S(2)}) async-start(bf16[16,16,2560]{2,1,0:T(8,128)(2,1)} %bitcast.88), calls=%async_computation.3 | async-start | bytes 2621440 | tf_op jit(solution)/shard_map/all_to_all | solution.py:21
  125.8 5.1 %copy-start.7 = (bf16[2560]{0:T(1024)(128)(2,1)S(1)}, bf16[2560]{0:T(1024)(128)(2,1)}, u32[]{:S(2)}) copy-start(bf16[2560]{0:T(1024)(128)(2,1)} %param.23) | copy-start | bytes 15364
  129.3 22.8 %collective-permute-start.6 = (bf16[64,2560]{1,0:T(8,128)(2,1)}, bf16[64,2560]{1,0:T(8,128)(2,1)S(1)}, u32[]{:S(2)}, u32[]{:S(2)}) collective-permute-start(bf16[64,2560]{1,0:T(8,128)(2,1)} %fusion.10), channel_id=1, source_target_pairs={{0,16},{1,17},{2,18},{3,19},{4,20},{5,21},{6,22},{7,23},{8,24},{9,... | collective-permute-start | bytes 983048 | tf_op jit(solution)/shard_map/ppermute | solution.py:148
  150.9 2.4 %copy-start.8 = (s32[1,64]{1,0:T(1,128)S(1)}, s32[1,64]{1,0:T(1,128)}, u32[]{:S(2)}) copy-start(s32[1,64]{1,0:T(1,128)} %param.16) | copy-start | bytes 772
  (1 other events, 0.7 us)

commit v5 on v4

--- a/solution.py
+++ b/solution.py
@@ -47,6 +47,17 @@
     zero = jnp.zeros((), jnp.bfloat16)
     flat = (token_count, side_experts * capacity)
     return tuple(jnp.where(taken, part[:, :, None], zero).reshape(flat) for part in (high, low))
+
+
+def with_context(rows, shard_rows, norm_gain):
+    feature_count = norm_gain.shape[0]
+    image_ids = jnp.arange(shard_rows.shape[0], dtype=jnp.int32).astype(jnp.float32)
+    named = rows[:, feature_count : feature_count + 1].astype(jnp.float32)
+    choose = (named == image_ids[None, :]).astype(jnp.bfloat16)
+    context = jnp.dot(choose, shard_rows, preferred_element_type=jnp.float32)
+    hidden = rows[:, :feature_count].astype(jnp.float32) + context
+    inverse = lax.rsqrt(jnp.mean(hidden * hidden, axis=-1, keepdims=True) + epsilon)
+    return hidden, (hidden * inverse * norm_gain.astype(jnp.float32)).astype(jnp.bfloat16)
 
 
 def fill_slots(taken, normed):
@@ -103,20 +114,12 @@
     pooled = (pooled_sum / math.sqrt(image_rows.shape[1])).astype(jnp.bfloat16)
     copies = jnp.broadcast_to(pooled[None], (device_count,) + pooled.shape)
     shard_rows = exchange(copies).reshape(-1, feature_count)
-    image_ids = jnp.arange(shard_rows.shape[0], dtype=jnp.int32)
-    choose = (response_image[:, None] == image_ids[None, :]).astype(jnp.bfloat16)
-    response_context = jnp.dot(choose, shard_rows, preferred_element_type=jnp.float32).astype(
-        jnp.bfloat16
-    )
     response_onehot = (
         token_response[0][:, None] == jnp.arange(response_count, dtype=jnp.int32)[None, :]
     )
-    token_context = jnp.dot(
-        response_onehot.astype(jnp.bfloat16), response_context, preferred_element_type=jnp.float32
-    )
-    hidden_state = text_rows.astype(jnp.float32) + token_context
-    inverse = lax.rsqrt(jnp.mean(hidden_state * hidden_state, axis=-1, keepdims=True) + epsilon)
-    normed = (hidden_state * inverse * norm_gain.astype(jnp.float32)).astype(jnp.bfloat16)
+    token_image = jnp.sum(jnp.where(response_onehot, response_image[None, :], 0), axis=1)
+    tag = jnp.broadcast_to(token_image[:, None], (token_count, 128)).astype(jnp.bfloat16)
+    rows = jnp.concatenate([text_rows, tag], axis=1)
     side_experts = expert_count // 2
     half = device_count // 2
     first_expert = (lax.axis_index("expert") // half) * side_experts
@@ -125,24 +128,33 @@
     swap = [(device, device ^ 1) for device in range(device_count)]
     weights = (gate_weight[0], up_weight[0], down_weight[0])
     far_routes = lax.ppermute(expert_routes, "expert", across)
-    far_normed = lax.ppermute(normed, "expert", across)
+    far_rows = lax.ppermute(rows, "expert", across)
     near_taken = slot_onehot(expert_routes, first_expert, side_experts, capacity)
     far_taken = slot_onehot(far_routes, first_expert, side_experts, capacity)
     slot_total = side_experts * capacity
+    flat = (slot_total, feature_count)
     blocks = (half, slot_total // half, feature_count)
-    flat = (slot_total, feature_count)
-    near_in = exchange(fill_slots(near_taken, normed).reshape(blocks), sides).reshape(flat)
-    far_slots = fill_slots(far_taken, far_normed).reshape(blocks)
-    near_in, far_slots = lax.optimization_barrier((near_in, far_slots))
+    tagged_flat = (slot_total, rows.shape[1])
+    tagged = (half, slot_total // half, rows.shape[1])
+    near_slots = fill_slots(near_taken, rows).reshape(tagged)
+    far_slots = fill_slots(far_taken, far_rows).reshape(tagged)
+    near_slots, far_slots, shard_rows = lax.optimization_barrier(
+        (near_slots, far_slots, shard_rows)
+    )
+    near_in = exchange(near_slots, sides).reshape(tagged_flat)
     near_in, far_slots = lax.optimization_barrier((both_cores(near_in, swap), far_slots))
-    far_in = exchange(far_slots, sides).reshape(flat)
-    near_parts = expert_half(near_in, *weights)
+    far_in = exchange(far_slots, sides).reshape(tagged_flat)
+    near_input = with_context(near_in, shard_rows, norm_gain)[1]
+    near_parts = expert_half(near_input, *weights)
     near_parts, far_in = lax.optimization_barrier((near_parts, far_in))
     near_sum = sum_cores(near_parts, swap)
-    far_sum = sum_cores(expert_half(both_cores(far_in, swap), *weights), swap)
+    far_input = with_context(both_cores(far_in, swap), shard_rows, norm_gain)[1]
+    far_sum = sum_cores(expert_half(far_input, *weights), swap)
     near_sum, far_sum = lax.optimization_barrier((near_sum, far_sum))
     far_out = exchange(far_sum.reshape(blocks), sides).reshape(flat)
     near_out = exchange(near_sum.reshape(blocks), sides).reshape(flat)
+    hidden_state, normed = with_context(rows, shard_rows, norm_gain)
+    far_normed = with_context(far_rows, shard_rows, norm_gain)[1]
     far_blend = slot_blend(far_taken, far_normed, far_routes, router_weight, first_expert)
     near_blend = slot_blend(near_taken, normed, expert_routes, router_weight, first_expert)
     far_mixture = lax.ppermute(mix(far_blend, far_out).astype(jnp.bfloat16), "expert", across)

time: 155 us -> 165 us (1.065)
  waiting for transfers between devices: 65.4 us -> 71.9 us
  matrix products: 29.7 us -> 26.8 us
  other arithmetic: 6.73 us -> 9.61 us
  starting transfers between devices: 22.8 us -> 25.1 us
    all_to_all x4, waiting for transfers between devices: 39.5 us -> 47.7 us  [exchange(): lax.all_to_all(blocks, 'expert', split_axis=0, concat_axis=0, axis_index_...]
    ppermute x1, waiting for transfers between devices: 21.8 us -> 18.2 us  [body(): far_rows = lax.ppermute(rows, 'expert', across)]
    dot_general x1 -> x4, matrix products: 1.52 us -> 4.91 us  [with_context(): context = jnp.dot(choose, shard_rows, preferred_element_type=jnp.float32)]
    dot_general x2, matrix products: 7.5 us -> 4.49 us  [expert_half(): lax.dot_general(inputs, gate_rows, contract, preferred_element_type=jnp.f...]
    ppermute x1, starting transfers between devices: 0.35 us -> 2.74 us  [body(): far_rows = lax.ppermute(rows, 'expert', across)]
    unnamed x30 -> x34, local copies, waits for them, and re-layouts: 3.03 us -> 5.07 us
    dot_general x2, matrix products: 2.38 us -> 0.6 us  [slot_blend(): logits = jnp.dot(normed, router_weight, preferred_element_type=jnp.float32)]
  transfers between devices with their start and end apart: 11 -> 11, of which waited for: 8 -> 7; matrix products, arithmetic and copies ran while one was open for 21% -> 22% of each run, Pallas kernels for 0% -> 0%
where the time goes in v5:
time: 165 us; the launch traced here: 164 us
  waiting for transfers between devices  71.9 us (44%)
  matrix products  26.8 us (16%)
  starting transfers between devices  25.1 us (15%)
  blocking collectives  23.2 us (14%)
  other arithmetic  9.61 us (6%)
  local copies, waits for them, and re-layouts  6.6 us (4%)
    all_to_all x4, waiting for transfers between devices, exchange(): lax.all_to_all(blocks, 'expert', split_axis=0, concat_axis=0, axis_index_...  47.7 us
    all_to_all x1, blocking collectives, exchange(): lax.all_to_all(blocks, 'expert', split_axis=0, concat_axis=0, axis_index_...  23.2 us
    ppermute x1, waiting for transfers between devices, body(): far_rows = lax.ppermute(rows, 'expert', across)  18.2 us
    all_to_all x4, starting transfers between devices, exchange(): lax.all_to_all(blocks, 'expert', split_axis=0, concat_axis=0, axis_index_...  16 us
    unnamed x34, local copies, waits for them, and re-layouts  5.07 us
    dot_general x4, matrix products, with_context(): context = jnp.dot(choose, shard_rows, preferred_element_type=jnp.float32)  4.91 us
    ppermute x2, waiting for transfers between devices, both_cores(): return jnp.concatenate([mine, lax.ppermute(mine, 'expert', swap)], axis=0)  4.7 us
    dot_general x2, matrix products, expert_half(): lax.dot_general(inputs, up_rows, contract, preferred_element_type=jnp.flo...  4.69 us
  transfers between devices with their start and end apart: 11, of which 7 were waited for; matrix products, arithmetic and copies ran while one was open for 22% of the time, Pallas kernels for 0%

profile of v5, /device:TPU:0, one launch (start us, length us, event | category | flops | bytes accessed | tf_op | source)
XLA Modules:
  0.0 164.2 jit_solution(8689315734946322890)
XLA Ops:
  0.6 4.1 %collective-permute-start = (s32[64,6]{0,1:T(8,128)}, s32[64,6]{0,1:T(8,128)S(1)}, u32[]{:S(2)}, u32[]{:S(2)}) collective-permute-start(s32[64,6]{0,1:T(8,128)} %param.19), channel_id=1, source_target_pairs={{0,16},{1,17},{2,18},{3,19},{4,20},{5,21},{6,22},{7,23},{8,24},{9,... | collective-permute-start | bytes 4616 | tf_op jit(solution)/shard_map/ppermute | solution.py:130
  6.8 3.8 %all-to-all-start = ((bf16[32,2,2560]{2,1,0:T(2,128)(2,1)}), bf16[32,2,2560]{2,1,0:T(2,128)(2,1)S(1)}, u32[]{:S(2)}, u32[]{:S(2)}) async-start(bf16[32,2,2560]{2,1,0:T(2,128)(2,1)} %broadcast_in_dim.62), calls=%async_computation | async-start | bytes 655360 | tf_op jit(solution)/shard_map/all_to_all | solution.py:21
  12.5 2.7 %collective-permute-start.1 = (bf16[64,2688]{1,0:T(8,128)(2,1)S(1)}, bf16[64,2688]{1,0:T(8,128)(2,1)S(1)}, u32[]{:S(2)}, u32[]{:S(2)}) collective-permute-start(bf16[64,2688]{1,0:T(8,128)(2,1)S(1)} %pad_maximum_fusion.1), channel_id=1, source_target_pairs={{0,16},{1,17},{2,18},{3,19},{4,20},{5,21},{6,22},{7,23},{8,24},{9,... | collective-permute-start | bytes 1032200 | tf_op jit(solution)/shard_map/ppermute | solution.py:131
  16.5 1.5 convolution_convert_fusion.3
  18.0 18.2 %collective-permute-done.1 = bf16[64,2688]{1,0:T(8,128)(2,1)S(1)} collective-permute-done((bf16[64,2688]{1,0:T(8,128)(2,1)S(1)}, bf16[64,2688]{1,0:T(8,128)(2,1)S(1)}, u32[]{:S(2)}, u32[]{:S(2)}) %collective-permute-start.1) | collective-permute-done | bytes 344096 | tf_op jit(solution)/shard_map/ppermute | solution.py:131
  36.2 1.6 convolution_convert_fusion.2
  38.0 23.2 %all_to_all.25 = bf16[16,16,2688]{2,1,0:T(8,128)(2,1)S(1)} all-to-all(bf16[16,16,2688]{2,1,0:T(8,128)(2,1)S(1)} %bitcast.83), channel_id=1, replica_groups={{0,1,2,3,4,5,6,7,8,9,10,11,12,13,14,15},{16,17,18,19,20,21,22,23,24,25,..., dimensions={0} | all-to-all | bytes 2752512 | tf_op jit(solution)/shard_map/all_to_all | solution.py:21
  61.2 3.1 %collective-permute-done.2 = bf16[256,2688]{1,0:T(8,128)(2,1)S(1)} collective-permute-done((bf16[256,2688]{1,0:T(8,128)(2,1)S(1)}, bf16[256,2688]{1,0:T(8,128)(2,1)S(1)}, u32[]{:S(2)}, u32[]{:S(2)}) %collective-permute-start.2) | collective-permute-done | bytes 1376288 | tf_op jit(solution)/shard_map/ppermute | solution.py:71
  64.6 4.6 %all-to-all-start.2 = ((bf16[16,16,2688]{2,1,0:T(8,128)(2,1)}), bf16[16,16,2688]{2,1,0:T(8,128)(2,1)}, u32[]{:S(2)}, u32[]{:S(2)}) async-start(bf16[16,16,2688]{2,1,0:T(8,128)(2,1)} %bitcast.82), calls=%async_computation.2 | async-start | bytes 2752512 | tf_op jit(solution)/shard_map/all_to_all | solution.py:21
  71.3 2.3 %fusion.8 = f32[512,768]{1,0:T(8,128)S(1)} fusion(bf16[1,768,2560]{2,1,0:T(8,128)(2,1)S(1)} %copy-done.10, f32[512,2560]{1,0:T(8,128)S(1)} %get-tuple-element.49, f32[2560]{0:T(1024)S(1)} %convert_element_type.174, f32[512]{0:T(512)S(1)} %add_rsqrt_fusion.1), kind=kOutput, calls=%fused_computation.16 | convolution fusion | flops 2017198080 | bytes 10760192 | tf_op jit(solution)/shard_map/dot_general | solution.py:13
  73.6 2.4 %multiply_convert_fusion.3 = bf16[512,768]{1,0:T(8,128)(2,1)S(1)} fusion(f32[512,768]{1,0:T(8,128)S(1)} %fusion.8, bf16[1,768,2560]{2,1,0:T(8,128)(2,1)S(1)} %copy-done.12, f32[512,2560]{1,0:T(8,128)S(1)} %get-tuple-element.49, f32[2560]{0:T(1024)S(1)} %convert_element_type.174, f32[512]{0:T(512)S(1)} %add_rsqrt_fusion.1), kind=kOutput, calls=%fused_computation.28 | convolution fusion | flops 2019557376 | bytes 11546624 | tf_op jit(solution)/shard_map/dot_general | solution.py:14
  76.0 2.2 %convolution_convert_fusion.1 = bf16[512,2560]{1,0:T(8,128)(2,1)S(1)} fusion(bf16[512,768]{1,0:T(8,128)(2,1)S(1)} %multiply_convert_fusion.3, bf16[1,768,2560]{2,1,0:T(8,128)(2,1)S(1)} %copy-done.14), kind=kOutput, calls=%fused_computation.7 | convolution fusion | flops 2014576640 | bytes 7340032 | tf_op jit(solution)/shard_map/dot_general | solution.py:17
  78.2 11.0 %all-to-all-done.2 = bf16[16,16,2688]{2,1,0:T(8,128)(2,1)} async-done(((bf16[16,16,2688]{2,1,0:T(8,128)(2,1)}), bf16[16,16,2688]{2,1,0:T(8,128)(2,1)}, u32[]{:S(2)}, u32[]{:S(2)}) %all-to-all-start.2) | async-done | bytes 1376288 | tf_op jit(solution)/shard_map/all_to_all | solution.py:21
  89.9 1.4 constant_dynamic-update-slice_fusion.1
  91.3 1.6 collective-permute-done.4
  96.4 2.2 %fusion.6 = f32[512,768]{1,0:T(8,128)S(1)} fusion(bf16[512,2560]{1,0:T(8,128)(2,1)S(1)} %multiply_convert_fusion, bf16[1,768,2560]{2,1,0:T(8,128)(2,1)S(1)} %copy-done.11), kind=kOutput, calls=%fused_computation.14 | convolution fusion | flops 2013265920 | bytes 8126464 | tf_op jit(solution)/shard_map/dot_general | solution.py:13
  98.6 2.3 %multiply_convert_fusion.2 = bf16[512,768]{1,0:T(8,128)(2,1)S(1)} fusion(f32[512,768]{1,0:T(8,128)S(1)} %fusion.6, bf16[512,2560]{1,0:T(8,128)(2,1)S(1)} %multiply_convert_fusion, bf16[1,768,2560]{2,1,0:T(8,128)(2,1)S(1)} %copy-done.13), kind=kOutput, calls=%fused_computation.27 | convolution fusion | flops 2015625216 | bytes 8912896 | tf_op jit(solution)/shard_map/dot_general | solution.py:14
  101.0 2.2 %convolution_convert_fusion = bf16[512,2560]{1,0:T(8,128)(2,1)S(1)} fusion(bf16[512,768]{1,0:T(8,128)(2,1)S(1)} %multiply_convert_fusion.2, bf16[1,768,2560]{2,1,0:T(8,128)(2,1)S(1)} %copy-done.15), kind=kOutput, calls=%fused_computation.6 | convolution fusion | flops 2014576640 | bytes 7340032 | tf_op jit(solution)/shard_map/dot_general | solution.py:17
  103.5 1.6 add_convert_fusion.1
  107.8 3.7 %all-to-all-start.4 = ((bf16[16,16,2560]{2,1,0:T(8,128)(2,1)}), bf16[16,16,2560]{2,1,0:T(8,128)(2,1)S(1)}, u32[]{:S(2)}, u32[]{:S(2)}) async-start(bf16[16,16,2560]{2,1,0:T(8,128)(2,1)} %bitcast.21), calls=%async_computation.4 | async-start | bytes 2621440 | tf_op jit(solution)/shard_map/all_to_all | solution.py:21
  112.4 18.4 %all-to-all-done.4 = bf16[16,16,2560]{2,1,0:T(8,128)(2,1)S(1)} async-done(((bf16[16,16,2560]{2,1,0:T(8,128)(2,1)}), bf16[16,16,2560]{2,1,0:T(8,128)(2,1)S(1)}, u32[]{:S(2)}, u32[]{:S(2)}) %all-to-all-start.4) | async-done | bytes 1310752 | tf_op jit(solution)/shard_map/all_to_all | solution.py:21
  130.8 3.9 %all-to-all-start.3 = ((bf16[16,16,2560]{2,1,0:T(8,128)(2,1)}), bf16[16,16,2560]{2,1,0:T(8,128)(2,1)S(1)}, u32[]{:S(2)}, u32[]{:S(2)}) async-start(bf16[16,16,2560]{2,1,0:T(8,128)(2,1)} %bitcast.86), calls=%async_computation.3 | async-start | bytes 2621440 | tf_op jit(solution)/shard_map/all_to_all | solution.py:21
  141.3 1.5 collective-permute-start.6
  142.8 18.3 %all-to-all-done.3 = bf16[16,16,2560]{2,1,0:T(8,128)(2,1)S(1)} async-done(((bf16[16,16,2560]{2,1,0:T(8,128)(2,1)}), bf16[16,16,2560]{2,1,0:T(8,128)(2,1)S(1)}, u32[]{:S(2)}, u32[]{:S(2)}) %all-to-all-start.3) | async-done | bytes 1310752 | tf_op jit(solution)/shard_map/all_to_all | solution.py:21
  (92 shorter events, 25.4 us)
Async XLA Ops:
  0.6 4.8 %copy-start = (bf16[2,16,2560]{2,1,0:T(8,128)(2,1)S(1)}, bf16[2,16,2560]{2,1,0:T(8,128)(2,1)}, u32[]{:S(2)}) copy-start(bf16[2,16,2560]{2,1,0:T(8,128)(2,1)} %param.13) | copy-start | bytes 491524
  0.6 14.7 %collective-permute-start = (s32[64,6]{0,1:T(8,128)}, s32[64,6]{0,1:T(8,128)S(1)}, u32[]{:S(2)}, u32[]{:S(2)}) collective-permute-start(s32[64,6]{0,1:T(8,128)} %param.19), channel_id=1, source_target_pairs={{0,16},{1,17},{2,18},{3,19},{4,20},{5,21},{6,22},{7,23},{8,24},{9,... | collective-permute-start | bytes 4616 | tf_op jit(solution)/shard_map/ppermute | solution.py:130
  6.8 31.0 %all-to-all-start = ((bf16[32,2,2560]{2,1,0:T(2,128)(2,1)}), bf16[32,2,2560]{2,1,0:T(2,128)(2,1)S(1)}, u32[]{:S(2)}, u32[]{:S(2)}) async-start(bf16[32,2,2560]{2,1,0:T(2,128)(2,1)} %broadcast_in_dim.62), calls=%async_computation | async-start | bytes 655360 | tf_op jit(solution)/shard_map/all_to_all | solution.py:21
  12.5 23.7 %collective-permute-start.1 = (bf16[64,2688]{1,0:T(8,128)(2,1)S(1)}, bf16[64,2688]{1,0:T(8,128)(2,1)S(1)}, u32[]{:S(2)}, u32[]{:S(2)}) collective-permute-start(bf16[64,2688]{1,0:T(8,128)(2,1)S(1)} %pad_maximum_fusion.1), channel_id=1, source_target_pairs={{0,16},{1,17},{2,18},{3,19},{4,20},{5,21},{6,22},{7,23},{8,24},{9,... | collective-permute-start | bytes 1032200 | tf_op jit(solution)/shard_map/ppermute | solution.py:131
  18.0 43.2 %copy-start.7 = (bf16[2560]{0:T(1024)(128)(2,1)S(1)}, bf16[2560]{0:T(1024)(128)(2,1)}, u32[]{:S(2)}) copy-start(bf16[2560]{0:T(1024)(128)(2,1)} %param.17) | copy-start | bytes 15364
  36.2 25.0 %copy-start.3 = (bf16[64,2688]{1,0:T(8,128)(2,1)}, bf16[64,2688]{1,0:T(8,128)(2,1)S(1)}, u32[]{:S(2)}) copy-start(bf16[64,2688]{1,0:T(8,128)(2,1)S(1)} %collective-permute-done.1) | copy-start | bytes 1032196
  61.2 3.1 %collective-permute-start.2 = (bf16[256,2688]{1,0:T(8,128)(2,1)S(1)}, bf16[256,2688]{1,0:T(8,128)(2,1)S(1)}, u32[]{:S(2)}, u32[]{:S(2)}) collective-permute-start(bf16[256,2688]{1,0:T(8,128)(2,1)S(1)} %bitcast.84), channel_id=1, source_target_pairs={{0,1},{1,0},{2,3},{3,2},{4,5},{5,4},{6,7},{7,6},{8,9},{9,8},{10,11... | collective-permute-start | bytes 4128776 | tf_op jit(solution)/shard_map/ppermute | solution.py:71
  64.6 24.6 %all-to-all-start.2 = ((bf16[16,16,2688]{2,1,0:T(8,128)(2,1)}), bf16[16,16,2688]{2,1,0:T(8,128)(2,1)}, u32[]{:S(2)}, u32[]{:S(2)}) async-start(bf16[16,16,2688]{2,1,0:T(8,128)(2,1)} %bitcast.82), calls=%async_computation.2 | async-start | bytes 2752512 | tf_op jit(solution)/shard_map/all_to_all | solution.py:21
  71.3 2.3 %copy-start.12 = (bf16[1,768,2560]{2,1,0:T(8,128)(2,1)S(1)}, bf16[1,768,2560]{2,1,0:T(8,128)(2,1)}, u32[]{:S(2)}) copy-start(bf16[1,768,2560]{2,1,0:T(8,128)(2,1)} %param.21) | copy-start | bytes 11796484
  73.6 2.4 %copy-start.14 = (bf16[1,768,2560]{2,1,0:T(8,128)(2,1)S(1)}, bf16[1,768,2560]{2,1,0:T(8,128)(2,1)}, u32[]{:S(2)}) copy-start(bf16[1,768,2560]{2,1,0:T(8,128)(2,1)} %param.22) | copy-start | bytes 11796484
  89.2 3.7 %collective-permute-start.4 = (bf16[256,2688]{1,0:T(8,128)(2,1)}, bf16[256,2688]{1,0:T(8,128)(2,1)S(1)}, u32[]{:S(2)}, u32[]{:S(2)}) collective-permute-start(bf16[256,2688]{1,0:T(8,128)(2,1)} %bitcast.16), channel_id=1, source_target_pairs={{0,1},{1,0},{2,3},{3,2},{4,5},{5,4},{6,7},{7,6},{8,9},{9,8},{10,11... | collective-permute-start | bytes 4128776 | tf_op jit(solution)/shard_map/ppermute | solution.py:71
  89.3 14.2 %collective-permute-start.3 = (bf16[256,2560]{1,0:T(8,128)(2,1)S(1)}, bf16[256,2560]{1,0:T(8,128)(2,1)S(1)}, u32[]{:S(2)}, u32[]{:S(2)}) collective-permute-start(bf16[256,2560]{1,0:T(8,128)(2,1)S(1)} %slice.34), channel_id=1, source_target_pairs={{0,1},{1,0},{2,3},{3,2},{4,5},{5,4},{6,7},{7,6},{8,9},{9,8},{10,11... | collective-permute-start | bytes 3932168 | tf_op jit(solution)/shard_map/ppermute | solution.py:76
  96.4 2.2 %copy-start.13 = (bf16[1,768,2560]{2,1,0:T(8,128)(2,1)S(1)}, bf16[1,768,2560]{2,1,0:T(8,128)(2,1)}, u32[]{:S(2)}) copy-start(bf16[1,768,2560]{2,1,0:T(8,128)(2,1)} %param.21) | copy-start | bytes 11796484
  98.6 2.3 %copy-start.15 = (bf16[1,768,2560]{2,1,0:T(8,128)(2,1)S(1)}, bf16[1,768,2560]{2,1,0:T(8,128)(2,1)}, u32[]{:S(2)}) copy-start(bf16[1,768,2560]{2,1,0:T(8,128)(2,1)} %param.22) | copy-start | bytes 11796484
  103.3 3.1 %collective-permute-start.5 = (bf16[256,2560]{1,0:T(8,128)(2,1)S(1)}, bf16[256,2560]{1,0:T(8,128)(2,1)S(1)}, u32[]{:S(2)}, u32[]{:S(2)}) collective-permute-start(bf16[256,2560]{1,0:T(8,128)(2,1)S(1)} %slice.44), channel_id=1, source_target_pairs={{0,1},{1,0},{2,3},{3,2},{4,5},{5,4},{6,7},{7,6},{8,9},{9,8},{10,11... | collective-permute-start | bytes 3932168 | tf_op jit(solution)/shard_map/ppermute | solution.py:76
  105.1 6.4 %copy-start.6 = (s32[64,6]{0,1:T(8,128)S(1)}, s32[64,6]{0,1:T(8,128)}, u32[]{:S(2)}) copy-start(s32[64,6]{0,1:T(8,128)} %param.19) | copy-start | bytes 4612
  107.8 23.0 %all-to-all-start.4 = ((bf16[16,16,2560]{2,1,0:T(8,128)(2,1)}), bf16[16,16,2560]{2,1,0:T(8,128)(2,1)S(1)}, u32[]{:S(2)}, u32[]{:S(2)}) async-start(bf16[16,16,2560]{2,1,0:T(8,128)(2,1)} %bitcast.21), calls=%async_computation.4 | async-start | bytes 2621440 | tf_op jit(solution)/shard_map/all_to_all | solution.py:21
  130.8 7.6 %copy-start.5 = (bf16[2560,16]{0,1:T(8,128)(2,1)S(1)}, bf16[2560,16]{0,1:T(8,128)(2,1)}, u32[]{:S(2)}) copy-start(bf16[2560,16]{0,1:T(8,128)(2,1)} %param.18) | copy-start | bytes 245764
  130.8 30.3 %all-to-all-start.3 = ((bf16[16,16,2560]{2,1,0:T(8,128)(2,1)}), bf16[16,16,2560]{2,1,0:T(8,128)(2,1)S(1)}, u32[]{:S(2)}, u32[]{:S(2)}) async-start(bf16[16,16,2560]{2,1,0:T(8,128)(2,1)} %bitcast.86), calls=%async_computation.3 | async-start | bytes 2621440 | tf_op jit(solution)/shard_map/all_to_all | solution.py:21
  134.7 4.0 %copy-start.4 = (bf16[64,2688]{1,0:T(8,128)(2,1)S(1)}, bf16[64,2688]{1,0:T(8,128)(2,1)}, u32[]{:S(2)}) copy-start(bf16[64,2688]{1,0:T(8,128)(2,1)} %copy-done.3) | copy-start | bytes 1032196
  139.0 3.7 %copy-start.8 = (bf16[2560]{0:T(1024)(128)(2,1)S(1)}, bf16[2560]{0:T(1024)(128)(2,1)}, u32[]{:S(2)}) copy-start(bf16[2560]{0:T(1024)(128)(2,1)} %param.23) | copy-start | bytes 15364
  140.2 22.1 %copy-start.2 = (f32[64,2560]{1,0:T(8,128)S(1)}, f32[64,2560]{1,0:T(8,128)}, u32[]{:S(2)}) copy-start(f32[64,2560]{1,0:T(8,128)} %copy-done.1) | copy-start | bytes 1966084
  141.3 21.0 %collective-permute-start.6 = (bf16[64,2560]{1,0:T(8,128)(2,1)}, bf16[64,2560]{1,0:T(8,128)(2,1)S(1)}, u32[]{:S(2)}, u32[]{:S(2)}) collective-permute-start(bf16[64,2560]{1,0:T(8,128)(2,1)} %fusion.10), channel_id=1, source_target_pairs={{0,16},{1,17},{2,18},{3,19},{4,20},{5,21},{6,22},{7,23},{8,24},{9,... | collective-permute-start | bytes 983048 | tf_op jit(solution)/shard_map/ppermute | solution.py:160
  161.1 2.5 %copy-start.9 = (s32[1,64]{1,0:T(1,128)S(1)}, s32[1,64]{1,0:T(1,128)}, u32[]{:S(2)}) copy-start(s32[1,64]{1,0:T(1,128)} %param.16) | copy-start | bytes 772
  (3 other events, 5.1 us)

commit v6 on v5

--- a/solution.py
+++ b/solution.py
@@ -138,10 +138,9 @@
     tagged = (half, slot_total // half, rows.shape[1])
     near_slots = fill_slots(near_taken, rows).reshape(tagged)
     far_slots = fill_slots(far_taken, far_rows).reshape(tagged)
-    near_slots, far_slots, shard_rows = lax.optimization_barrier(
-        (near_slots, far_slots, shard_rows)
-    )
+    near_slots, shard_rows = lax.optimization_barrier((near_slots, shard_rows))
     near_in = exchange(near_slots, sides).reshape(tagged_flat)
+    near_in, far_slots = lax.optimization_barrier((near_in, far_slots))
     near_in, far_slots = lax.optimization_barrier((both_cores(near_in, swap), far_slots))
     far_in = exchange(far_slots, sides).reshape(tagged_flat)
     near_input = with_context(near_in, shard_rows, norm_gain)[1]

time: 165 us -> 160 us (0.970)
  blocking collectives: 23.2 us -> 0 us
  waiting for transfers between devices: 71.9 us -> 87.1 us
    all_to_all x1 -> x0, blocking collectives: 23.2 us -> none  [exchange(): lax.all_to_all(blocks, 'expert', split_axis=0, concat_axis=0, axis_index_...]
    all_to_all x4 -> x5, waiting for transfers between devices: 47.7 us -> 57.9 us  [exchange(): lax.all_to_all(blocks, 'expert', split_axis=0, concat_axis=0, axis_index_...]
    ppermute x1, waiting for transfers between devices: 18.2 us -> 23 us  [body(): far_rows = lax.ppermute(rows, 'expert', across)]
    all_to_all x4 -> x5, starting transfers between devices: 16 us -> 20.4 us  [exchange(): lax.all_to_all(blocks, 'expert', split_axis=0, concat_axis=0, axis_index_...]
    ppermute x1, starting transfers between devices: 2.74 us -> 0.07 us  [body(): far_rows = lax.ppermute(rows, 'expert', across)]
    unnamed x34 -> x36, local copies, waits for them, and re-layouts: 5.07 us -> 5.07 us
  transfers between devices with their start and end apart: 11 -> 12, of which waited for: 7 -> 9; matrix products, arithmetic and copies ran while one was open for 22% -> 23% of each run, Pallas kernels for 0% -> 0%
where the time goes in v6:
time: 160 us; the launch traced here: 159 us
  waiting for transfers between devices  87.1 us (54%)
  matrix products  27.8 us (17%)
  starting transfers between devices  26.3 us (16%)
  other arithmetic  9.97 us (6%)
  local copies, waits for them, and re-layouts  6.6 us (4%)
    all_to_all x5, waiting for transfers between devices, exchange(): lax.all_to_all(blocks, 'expert', split_axis=0, concat_axis=0, axis_index_...  57.9 us
    ppermute x1, waiting for transfers between devices, body(): far_rows = lax.ppermute(rows, 'expert', across)  23 us
    all_to_all x5, starting transfers between devices, exchange(): lax.all_to_all(blocks, 'expert', split_axis=0, concat_axis=0, axis_index_...  20.4 us
    unnamed x36, local copies, waits for them, and re-layouts  5.07 us
    ppermute x2, waiting for transfers between devices, both_cores(): return jnp.concatenate([mine, lax.ppermute(mine, 'expert', swap)], axis=0)  4.91 us
    dot_general x4, matrix products, with_context(): context = jnp.dot(choose, shard_rows, preferred_element_type=jnp.float32)  4.9 us
    dot_general x2, matrix products, expert_half(): lax.dot_general(inputs, up_rows, contract, preferred_element_type=jnp.flo...  4.68 us
    dot_general x2, matrix products, expert_half(): lax.dot_general(inputs, gate_rows, contract, preferred_element_type=jnp.f...  4.48 us
  transfers between devices with their start and end apart: 12, of which 9 were waited for; matrix products, arithmetic and copies ran while one was open for 23% of the time, Pallas kernels for 0%

profile of v6, /device:TPU:0, one launch (start us, length us, event | category | flops | bytes accessed | tf_op | source)
XLA Modules:
  0.0 158.9 jit_solution(17531497056198153028)
XLA Ops:
  0.6 4.1 %collective-permute-start = (s32[64,6]{0,1:T(8,128)}, s32[64,6]{0,1:T(8,128)S(1)}, u32[]{:S(2)}, u32[]{:S(2)}) collective-permute-start(s32[64,6]{0,1:T(8,128)} %param.19), channel_id=1, source_target_pairs={{0,16},{1,17},{2,18},{3,19},{4,20},{5,21},{6,22},{7,23},{8,24},{9,... | collective-permute-start | bytes 4616 | tf_op jit(solution)/shard_map/ppermute | solution.py:130
  6.8 3.8 %all-to-all-start = ((bf16[32,2,2560]{2,1,0:T(2,128)(2,1)}), bf16[32,2,2560]{2,1,0:T(2,128)(2,1)S(1)}, u32[]{:S(2)}, u32[]{:S(2)}) async-start(bf16[32,2,2560]{2,1,0:T(2,128)(2,1)} %broadcast_in_dim.62), calls=%async_computation | async-start | bytes 655360 | tf_op jit(solution)/shard_map/all_to_all | solution.py:21
  12.8 2.5 %convolution_convert_fusion.3 = bf16[256,2688]{1,0:T(8,128)(2,1)} fusion(pred[64,256]{0,1:T(32,128)(4,1)S(1)} %get-tuple-element.37, bf16[64,128]{1,0:T(8,128)(2,1)S(1)} %broadcast_in_dim.61, bf16[64,2560]{1,0:T(8,128)(2,1)} %param.12), kind=kOutput, calls=%fused_computation.19 | convolution fusion | flops 89456640 | bytes 1736704 | tf_op jit(solution)/shard_map/dot_general | solution.py:65
  15.4 7.3 %all-to-all-done = bf16[32,2,2560]{2,1,0:T(2,128)(2,1)S(1)} async-done(((bf16[32,2,2560]{2,1,0:T(2,128)(2,1)}), bf16[32,2,2560]{2,1,0:T(2,128)(2,1)S(1)}, u32[]{:S(2)}, u32[]{:S(2)}) %all-to-all-start) | async-done | bytes 327712 | tf_op jit(solution)/shard_map/all_to_all | solution.py:21
  22.8 4.4 %all-to-all-start.1 = ((bf16[16,16,2688]{2,1,0:T(8,128)(2,1)}), bf16[16,16,2688]{2,1,0:T(8,128)(2,1)}, u32[]{:S(2)}, u32[]{:S(2)}) async-start(bf16[16,16,2688]{2,1,0:T(8,128)(2,1)} %bitcast.3), calls=%async_computation.1 | async-start | bytes 2752512 | tf_op jit(solution)/shard_map/all_to_all | solution.py:21
  27.3 23.0 %collective-permute-done.1 = bf16[64,2688]{1,0:T(8,128)(2,1)S(1)} collective-permute-done((bf16[64,2688]{1,0:T(8,128)(2,1)S(1)}, bf16[64,2688]{1,0:T(8,128)(2,1)S(1)}, u32[]{:S(2)}, u32[]{:S(2)}) %collective-permute-start.1) | collective-permute-done | bytes 344096 | tf_op jit(solution)/shard_map/ppermute | solution.py:131
  50.3 1.6 %convolution_convert_fusion.2 = bf16[256,2688]{1,0:T(8,128)(2,1)} fusion(pred[64,256]{0,1:T(32,128)(4,1)S(1)} %get-tuple-element.36, bf16[64,2688]{1,0:T(8,128)(2,1)S(1)} %collective-permute-done.1), kind=kOutput, calls=%fused_computation.18 | convolution fusion | flops 88768512 | bytes 1736704 | tf_op jit(solution)/shard_map/dot_general | solution.py:65
  51.9 2.4 %all-to-all-done.1 = bf16[16,16,2688]{2,1,0:T(8,128)(2,1)} async-done(((bf16[16,16,2688]{2,1,0:T(8,128)(2,1)}), bf16[16,16,2688]{2,1,0:T(8,128)(2,1)}, u32[]{:S(2)}, u32[]{:S(2)}) %all-to-all-start.1) | async-done | bytes 1376288 | tf_op jit(solution)/shard_map/all_to_all | solution.py:21
  54.4 3.3 %collective-permute-done.2 = bf16[256,2688]{1,0:T(8,128)(2,1)S(1)} collective-permute-done((bf16[256,2688]{1,0:T(8,128)(2,1)}, bf16[256,2688]{1,0:T(8,128)(2,1)S(1)}, u32[]{:S(2)}, u32[]{:S(2)}) %collective-permute-start.2) | collective-permute-done | bytes 1376288 | tf_op jit(solution)/shard_map/ppermute | solution.py:71
  57.7 1.5 pad_maximum_fusion
  59.3 4.6 %all-to-all-start.2 = ((bf16[16,16,2688]{2,1,0:T(8,128)(2,1)}), bf16[16,16,2688]{2,1,0:T(8,128)(2,1)}, u32[]{:S(2)}, u32[]{:S(2)}) async-start(bf16[16,16,2688]{2,1,0:T(8,128)(2,1)} %bitcast.82), calls=%async_computation.2 | async-start | bytes 2752512 | tf_op jit(solution)/shard_map/all_to_all | solution.py:21
  66.0 2.3 %fusion.8 = f32[512,768]{1,0:T(8,128)S(1)} fusion(bf16[1,768,2560]{2,1,0:T(8,128)(2,1)S(1)} %copy-done.11, f32[512,2560]{1,0:T(8,128)S(1)} %get-tuple-element.51, f32[2560]{0:T(1024)S(1)} %convert_element_type.173, f32[512]{0:T(512)S(1)} %add_rsqrt_fusion.1), kind=kOutput, calls=%fused_computation.16 | convolution fusion | flops 2017198080 | bytes 10760192 | tf_op jit(solution)/shard_map/dot_general | solution.py:13
  68.3 2.4 %multiply_convert_fusion.3 = bf16[512,768]{1,0:T(8,128)(2,1)S(1)} fusion(f32[512,768]{1,0:T(8,128)S(1)} %fusion.8, bf16[1,768,2560]{2,1,0:T(8,128)(2,1)S(1)} %copy-done.13, f32[512,2560]{1,0:T(8,128)S(1)} %get-tuple-element.51, f32[2560]{0:T(1024)S(1)} %convert_element_type.173, f32[512]{0:T(512)S(1)} %add_rsqrt_fusion.1), kind=kOutput, calls=%fused_computation.28 | convolution fusion | flops 2019557376 | bytes 11546624 | tf_op jit(solution)/shard_map/dot_general | solution.py:14
  70.7 2.2 %convolution_convert_fusion.1 = bf16[512,2560]{1,0:T(8,128)(2,1)S(1)} fusion(bf16[512,768]{1,0:T(8,128)(2,1)S(1)} %multiply_convert_fusion.3, bf16[1,768,2560]{2,1,0:T(8,128)(2,1)S(1)} %copy-done.15), kind=kOutput, calls=%fused_computation.7 | convolution fusion | flops 2014576640 | bytes 7340032 | tf_op jit(solution)/shard_map/dot_general | solution.py:17
  72.9 11.0 %all-to-all-done.2 = bf16[16,16,2688]{2,1,0:T(8,128)(2,1)} async-done(((bf16[16,16,2688]{2,1,0:T(8,128)(2,1)}), bf16[16,16,2688]{2,1,0:T(8,128)(2,1)}, u32[]{:S(2)}, u32[]{:S(2)}) %all-to-all-start.2) | async-done | bytes 1376288 | tf_op jit(solution)/shard_map/all_to_all | solution.py:21
  86.0 1.6 %collective-permute-done.4 = bf16[256,2688]{1,0:T(8,128)(2,1)S(1)} collective-permute-done((bf16[256,2688]{1,0:T(8,128)(2,1)}, bf16[256,2688]{1,0:T(8,128)(2,1)S(1)}, u32[]{:S(2)}, u32[]{:S(2)}) %collective-permute-start.4) | collective-permute-done | bytes 1376288 | tf_op jit(solution)/shard_map/ppermute | solution.py:71
  91.1 2.2 %fusion.6 = f32[512,768]{1,0:T(8,128)S(1)} fusion(bf16[512,2560]{1,0:T(8,128)(2,1)S(1)} %multiply_convert_fusion, bf16[1,768,2560]{2,1,0:T(8,128)(2,1)S(1)} %copy-done.12), kind=kOutput, calls=%fused_computation.14 | convolution fusion | flops 2013265920 | bytes 8126464 | tf_op jit(solution)/shard_map/dot_general | solution.py:13
  93.3 2.3 %multiply_convert_fusion.2 = bf16[512,768]{1,0:T(8,128)(2,1)S(1)} fusion(f32[512,768]{1,0:T(8,128)S(1)} %fusion.6, bf16[512,2560]{1,0:T(8,128)(2,1)S(1)} %multiply_convert_fusion, bf16[1,768,2560]{2,1,0:T(8,128)(2,1)S(1)} %copy-done.14), kind=kOutput, calls=%fused_computation.27 | convolution fusion | flops 2015625216 | bytes 8912896 | tf_op jit(solution)/shard_map/dot_general | solution.py:14
  95.7 2.2 %convolution_convert_fusion = bf16[512,2560]{1,0:T(8,128)(2,1)S(1)} fusion(bf16[512,768]{1,0:T(8,128)(2,1)S(1)} %multiply_convert_fusion.2, bf16[1,768,2560]{2,1,0:T(8,128)(2,1)S(1)} %copy-done.16), kind=kOutput, calls=%fused_computation.6 | convolution fusion | flops 2014576640 | bytes 7340032 | tf_op jit(solution)/shard_map/dot_general | solution.py:17
  98.2 1.6 %add_convert_fusion.1 = bf16[256,2560]{1,0:T(8,128)(2,1)} fusion(bf16[256,2560]{1,0:T(8,128)(2,1)S(1)} %collective-permute-done.3, bf16[512,2560]{1,0:T(8,128)(2,1)S(1)} %convolution_convert_fusion.1), kind=kLoop, calls=%fused_computation.26 | loop fusion | flops 2621440 | bytes 3932160 | tf_op jit(solution)/shard_map/convert_element_type | solution.py:77
  102.5 3.7 %all-to-all-start.4 = ((bf16[16,16,2560]{2,1,0:T(8,128)(2,1)}), bf16[16,16,2560]{2,1,0:T(8,128)(2,1)S(1)}, u32[]{:S(2)}, u32[]{:S(2)}) async-start(bf16[16,16,2560]{2,1,0:T(8,128)(2,1)} %bitcast.21), calls=%async_computation.4 | async-start | bytes 2621440 | tf_op jit(solution)/shard_map/all_to_all | solution.py:21
  107.0 18.4 %all-to-all-done.4 = bf16[16,16,2560]{2,1,0:T(8,128)(2,1)S(1)} async-done(((bf16[16,16,2560]{2,1,0:T(8,128)(2,1)}), bf16[16,16,2560]{2,1,0:T(8,128)(2,1)S(1)}, u32[]{:S(2)}, u32[]{:S(2)}) %all-to-all-start.4) | async-done | bytes 1310752 | tf_op jit(solution)/shard_map/all_to_all | solution.py:21
  125.5 3.9 %all-to-all-start.3 = ((bf16[16,16,2560]{2,1,0:T(8,128)(2,1)}), bf16[16,16,2560]{2,1,0:T(8,128)(2,1)S(1)}, u32[]{:S(2)}, u32[]{:S(2)}) async-start(bf16[16,16,2560]{2,1,0:T(8,128)(2,1)} %bitcast.83), calls=%async_computation.3 | async-start | bytes 2621440 | tf_op jit(solution)/shard_map/all_to_all | solution.py:21
  137.0 18.8 %all-to-all-done.3 = bf16[16,16,2560]{2,1,0:T(8,128)(2,1)S(1)} async-done(((bf16[16,16,2560]{2,1,0:T(8,128)(2,1)}), bf16[16,16,2560]{2,1,0:T(8,128)(2,1)S(1)}, u32[]{:S(2)}, u32[]{:S(2)}) %all-to-all-start.3) | async-done | bytes 1310752 | tf_op jit(solution)/shard_map/all_to_all | solution.py:21
  (95 shorter events, 26.7 us)
Async XLA Ops:
  0.6 4.8 %copy-start = (bf16[2,16,2560]{2,1,0:T(8,128)(2,1)S(1)}, bf16[2,16,2560]{2,1,0:T(8,128)(2,1)}, u32[]{:S(2)}) copy-start(bf16[2,16,2560]{2,1,0:T(8,128)(2,1)} %param.13) | copy-start | bytes 491524
  0.6 10.9 %collective-permute-start = (s32[64,6]{0,1:T(8,128)}, s32[64,6]{0,1:T(8,128)S(1)}, u32[]{:S(2)}, u32[]{:S(2)}) collective-permute-start(s32[64,6]{0,1:T(8,128)} %param.19), channel_id=1, source_target_pairs={{0,16},{1,17},{2,18},{3,19},{4,20},{5,21},{6,22},{7,23},{8,24},{9,... | collective-permute-start | bytes 4616 | tf_op jit(solution)/shard_map/ppermute | solution.py:130
  6.8 15.8 %all-to-all-start = ((bf16[32,2,2560]{2,1,0:T(2,128)(2,1)}), bf16[32,2,2560]{2,1,0:T(2,128)(2,1)S(1)}, u32[]{:S(2)}, u32[]{:S(2)}) async-start(bf16[32,2,2560]{2,1,0:T(2,128)(2,1)} %broadcast_in_dim.62), calls=%async_computation | async-start | bytes 655360 | tf_op jit(solution)/shard_map/all_to_all | solution.py:21
  12.6 14.6 %copy-start.5 = (bf16[64,2560]{1,0:T(8,128)(2,1)S(1)}, bf16[64,2560]{1,0:T(8,128)(2,1)}, u32[]{:S(2)}) copy-start(bf16[64,2560]{1,0:T(8,128)(2,1)} %param.12) | copy-start | bytes 983044
  22.8 31.5 %copy-start.8 = (bf16[2560]{0:T(1024)(128)(2,1)S(1)}, bf16[2560]{0:T(1024)(128)(2,1)}, u32[]{:S(2)}) copy-start(bf16[2560]{0:T(1024)(128)(2,1)} %param.17) | copy-start | bytes 15364
  22.8 31.5 %all-to-all-start.1 = ((bf16[16,16,2688]{2,1,0:T(8,128)(2,1)}), bf16[16,16,2688]{2,1,0:T(8,128)(2,1)}, u32[]{:S(2)}, u32[]{:S(2)}) async-start(bf16[16,16,2688]{2,1,0:T(8,128)(2,1)} %bitcast.3), calls=%async_computation.1 | async-start | bytes 2752512 | tf_op jit(solution)/shard_map/all_to_all | solution.py:21
  27.3 23.1 %collective-permute-start.1 = (bf16[64,2688]{1,0:T(8,128)(2,1)S(1)}, bf16[64,2688]{1,0:T(8,128)(2,1)S(1)}, u32[]{:S(2)}, u32[]{:S(2)}) collective-permute-start(bf16[64,2688]{1,0:T(8,128)(2,1)S(1)} %pad_maximum_fusion.1), channel_id=1, source_target_pairs={{0,16},{1,17},{2,18},{3,19},{4,20},{5,21},{6,22},{7,23},{8,24},{9,... | collective-permute-start | bytes 1032200 | tf_op jit(solution)/shard_map/ppermute | solution.py:131
  50.3 4.0 %copy-start.3 = (bf16[64,2688]{1,0:T(8,128)(2,1)}, bf16[64,2688]{1,0:T(8,128)(2,1)S(1)}, u32[]{:S(2)}) copy-start(bf16[64,2688]{1,0:T(8,128)(2,1)S(1)} %collective-permute-done.1) | copy-start | bytes 1032196
  54.3 3.3 %collective-permute-start.2 = (bf16[256,2688]{1,0:T(8,128)(2,1)}, bf16[256,2688]{1,0:T(8,128)(2,1)S(1)}, u32[]{:S(2)}, u32[]{:S(2)}) collective-permute-start(bf16[256,2688]{1,0:T(8,128)(2,1)} %bitcast.9), channel_id=1, source_target_pairs={{0,1},{1,0},{2,3},{3,2},{4,5},{5,4},{6,7},{7,6},{8,9},{9,8},{10,11... | collective-permute-start | bytes 4128776 | tf_op jit(solution)/shard_map/ppermute | solution.py:71
  59.3 24.6 %all-to-all-start.2 = ((bf16[16,16,2688]{2,1,0:T(8,128)(2,1)}), bf16[16,16,2688]{2,1,0:T(8,128)(2,1)}, u32[]{:S(2)}, u32[]{:S(2)}) async-start(bf16[16,16,2688]{2,1,0:T(8,128)(2,1)} %bitcast.82), calls=%async_computation.2 | async-start | bytes 2752512 | tf_op jit(solution)/shard_map/all_to_all | solution.py:21
  68.3 2.4 %copy-start.15 = (bf16[1,768,2560]{2,1,0:T(8,128)(2,1)S(1)}, bf16[1,768,2560]{2,1,0:T(8,128)(2,1)}, u32[]{:S(2)}) copy-start(bf16[1,768,2560]{2,1,0:T(8,128)(2,1)} %param.22) | copy-start | bytes 11796484
  83.9 3.7 %collective-permute-start.4 = (bf16[256,2688]{1,0:T(8,128)(2,1)}, bf16[256,2688]{1,0:T(8,128)(2,1)S(1)}, u32[]{:S(2)}, u32[]{:S(2)}) collective-permute-start(bf16[256,2688]{1,0:T(8,128)(2,1)} %bitcast.16), channel_id=1, source_target_pairs={{0,1},{1,0},{2,3},{3,2},{4,5},{5,4},{6,7},{7,6},{8,9},{9,8},{10,11... | collective-permute-start | bytes 4128776 | tf_op jit(solution)/shard_map/ppermute | solution.py:71
  84.0 14.2 %collective-permute-start.3 = (bf16[256,2560]{1,0:T(8,128)(2,1)S(1)}, bf16[256,2560]{1,0:T(8,128)(2,1)S(1)}, u32[]{:S(2)}, u32[]{:S(2)}) collective-permute-start(bf16[256,2560]{1,0:T(8,128)(2,1)S(1)} %slice.34), channel_id=1, source_target_pairs={{0,1},{1,0},{2,3},{3,2},{4,5},{5,4},{6,7},{7,6},{8,9},{9,8},{10,11... | collective-permute-start | bytes 3932168 | tf_op jit(solution)/shard_map/ppermute | solution.py:76
  93.3 2.3 %copy-start.16 = (bf16[1,768,2560]{2,1,0:T(8,128)(2,1)S(1)}, bf16[1,768,2560]{2,1,0:T(8,128)(2,1)}, u32[]{:S(2)}) copy-start(bf16[1,768,2560]{2,1,0:T(8,128)(2,1)} %param.22) | copy-start | bytes 11796484
  98.0 3.1 %collective-permute-start.5 = (bf16[256,2560]{1,0:T(8,128)(2,1)S(1)}, bf16[256,2560]{1,0:T(8,128)(2,1)S(1)}, u32[]{:S(2)}, u32[]{:S(2)}) collective-permute-start(bf16[256,2560]{1,0:T(8,128)(2,1)S(1)} %slice.44), channel_id=1, source_target_pairs={{0,1},{1,0},{2,3},{3,2},{4,5},{5,4},{6,7},{7,6},{8,9},{9,8},{10,11... | collective-permute-start | bytes 3932168 | tf_op jit(solution)/shard_map/ppermute | solution.py:76
  99.8 6.4 %copy-start.7 = (s32[64,6]{0,1:T(8,128)S(1)}, s32[64,6]{0,1:T(8,128)}, u32[]{:S(2)}) copy-start(s32[64,6]{0,1:T(8,128)} %param.19) | copy-start | bytes 4612
  102.5 23.0 %all-to-all-start.4 = ((bf16[16,16,2560]{2,1,0:T(8,128)(2,1)}), bf16[16,16,2560]{2,1,0:T(8,128)(2,1)S(1)}, u32[]{:S(2)}, u32[]{:S(2)}) async-start(bf16[16,16,2560]{2,1,0:T(8,128)(2,1)} %bitcast.21), calls=%async_computation.4 | async-start | bytes 2621440 | tf_op jit(solution)/shard_map/all_to_all | solution.py:21
  125.5 7.6 %copy-start.6 = (bf16[2560,16]{0,1:T(8,128)(2,1)S(1)}, bf16[2560,16]{0,1:T(8,128)(2,1)}, u32[]{:S(2)}) copy-start(bf16[2560,16]{0,1:T(8,128)(2,1)} %param.18) | copy-start | bytes 245764
  125.5 30.3 %all-to-all-start.3 = ((bf16[16,16,2560]{2,1,0:T(8,128)(2,1)}), bf16[16,16,2560]{2,1,0:T(8,128)(2,1)S(1)}, u32[]{:S(2)}, u32[]{:S(2)}) async-start(bf16[16,16,2560]{2,1,0:T(8,128)(2,1)} %bitcast.83), calls=%async_computation.3 | async-start | bytes 2621440 | tf_op jit(solution)/shard_map/all_to_all | solution.py:21
  129.4 4.0 %copy-start.4 = (bf16[64,2688]{1,0:T(8,128)(2,1)S(1)}, bf16[64,2688]{1,0:T(8,128)(2,1)}, u32[]{:S(2)}) copy-start(bf16[64,2688]{1,0:T(8,128)(2,1)} %copy-done.3) | copy-start | bytes 1032196
  133.7 3.3 %copy-start.9 = (bf16[2560]{0:T(1024)(128)(2,1)S(1)}, bf16[2560]{0:T(1024)(128)(2,1)}, u32[]{:S(2)}) copy-start(bf16[2560]{0:T(1024)(128)(2,1)} %param.23) | copy-start | bytes 15364
  134.9 22.1 %copy-start.2 = (f32[64,2560]{1,0:T(8,128)S(1)}, f32[64,2560]{1,0:T(8,128)}, u32[]{:S(2)}) copy-start(f32[64,2560]{1,0:T(8,128)} %copy-done.1) | copy-start | bytes 1966084
  136.0 21.0 %collective-permute-start.6 = (bf16[64,2560]{1,0:T(8,128)(2,1)}, bf16[64,2560]{1,0:T(8,128)(2,1)S(1)}, u32[]{:S(2)}, u32[]{:S(2)}) collective-permute-start(bf16[64,2560]{1,0:T(8,128)(2,1)} %fusion.10), channel_id=1, source_target_pairs={{0,16},{1,17},{2,18},{3,19},{4,20},{5,21},{6,22},{7,23},{8,24},{9,... | collective-permute-start | bytes 983048 | tf_op jit(solution)/shard_map/ppermute | solution.py:159
  155.8 2.5 %copy-start.10 = (s32[1,64]{1,0:T(1,128)S(1)}, s32[1,64]{1,0:T(1,128)}, u32[]{:S(2)}) copy-start(s32[1,64]{1,0:T(1,128)} %param.16) | copy-start | bytes 772
  (5 other events, 9.6 us)
